TPU v7x, 32 devices: a whole 2x2x4 slice. The times are simulated.
32 devices in a mesh: box: 16 (over z, y, core), tx: 2 (over x).
Axes of the slice: x: 2, y: 2, z: 4, core: 2. Of those that a mesh axis runs over, the one named last changes fastest.
Arguments:
- bank: bfloat16 [512, 512, 1024], P('box', 'tx'), may hold values from -6 to 6
- pick: int32 [32], replicated, may hold values from 0 to 511, as said below
- slot_box: int32 [512], replicated, may hold values from 0 to 511, each once
- leaf_factor: bfloat16 [512, 512, 128], P('box'), may hold values from -0.1875 to 0.1875
- self_factor: bfloat16 [9, 512, 64, 128], P(None, 'box'), may hold values from -0.375 to 0.375
- cross_factor: bfloat16 [9, 512, 64, 128], P(None, 'box'), may hold values from -0.375 to 0.375
- target_factor: bfloat16 [512, 64, 4096], P('box'), may hold values from -0.5 to 0.5
Outputs:
- field: bfloat16 [512, 32, 4096], P('box', 'tx')
Inputs may be any that keep to these rules, and one draw needn't show every extreme that they name: `pick`: distinct stored transmitters. `slot_box`: each box once.
All inputs are finite; a program needn't handle non-finite values.
Results may differ from a plain program's by a relative error of at most 0.023.
Values may be sent and summed in bfloat16 or wider, within the bound.
No kernel may reach another device: no remote copies, remote signals or barrier semaphores. Data moves between devices by JAX's collectives and lax.ppermute only.
A program may use at most 128 MiB of HBM per device.

v0:
```python
import jax
import jax.numpy as jnp
from jax import lax
from jax.sharding import PartitionSpec as P


def partner_2(block, axis, bit):
    count = lax.axis_size(axis)
    route = []
    for low in range(count):
        high = low | 1 << bit
        if high != low and high < count:
            route += [(low, high), (high, low)]
    return lax.ppermute(block, axis, route)


def complex_times(values, matrix):
    inner = matrix.shape[-2]
    half = matrix.shape[-1] // 2
    first = jnp.einsum(
        "brn,bnk->brk", values[..., :inner], matrix, preferred_element_type=jnp.float32
    )
    second = jnp.einsum(
        "brn,bnk->brk", values[..., inner:], matrix, preferred_element_type=jnp.float32
    )
    return jnp.concatenate(
        [first[..., :half] - second[..., half:], first[..., half:] + second[..., :half]], axis=-1
    )


def per_device(bank, pick, slot_box, leaf_factor, self_factor, cross_factor, target_factor):
    box_dev = bank.shape[0]
    bank_dev = bank.shape[1]
    tx_index = lax.axis_index("tx")
    local_pick = pick - tx_index * bank_dev
    chooser = (local_pick[:, None] == jnp.arange(bank_dev, dtype=jnp.int32)[None, :]).astype(
        jnp.bfloat16
    )
    picked = jnp.einsum("pj,bju->bpu", chooser, bank, preferred_element_type=jnp.float32)
    owned = lax.psum_scatter(picked.astype(jnp.bfloat16), "tx", scatter_dimension=1, tiled=True)
    coefs = complex_times(owned, leaf_factor).astype(jnp.bfloat16)
    box_index = lax.axis_index("box")
    sources = lax.dynamic_slice_in_dim(slot_box, box_index * box_dev, box_dev)
    piece = lax.all_gather(coefs, "box", axis=0, tiled=True)
    count = piece.shape[0]
    taker = (sources[:, None] == jnp.arange(count, dtype=jnp.int32)[None, :]).astype(jnp.bfloat16)
    current = jnp.einsum("sn,nrk->srk", taker, piece, preferred_element_type=jnp.float32).astype(
        jnp.bfloat16
    )
    levels = self_factor.shape[0]
    local_bits = box_dev.bit_length() - 1
    for level in range(levels):
        if level < local_bits:
            span = 1 << level
            shaped = current.reshape(
                box_dev // (2 * span), 2, span, current.shape[1], current.shape[2]
            )
            partner = jnp.flip(shaped, axis=1).reshape(current.shape)
        else:
            partner = partner_2(current, "box", level - local_bits)
        mixed = complex_times(current, self_factor[level]) + complex_times(
            partner, cross_factor[level]
        )
        current = mixed.astype(jnp.bfloat16)
    return complex_times(current, target_factor).astype(jnp.bfloat16)


def solution(mesh):
    in_specs = (
        P("box", "tx", None),
        P(),
        P(),
        P("box", None, None),
        P(None, "box", None, None),
        P(None, "box", None, None),
        P("box", None, None),
    )
    out_specs = P("box", "tx", None)
    return jax.shard_map(
        per_device, mesh=mesh, in_specs=in_specs, out_specs=out_specs, check_vma=False
    )
```

profile of v0, /device:TPU:0, one launch (start us, length us, event | category | flops | bytes accessed | tf_op | source)
XLA Modules:
  0.0 181.8 jit_solution(7554986634906261845)
XLA Ops:
  7.2 10.1 %convert_bitcast_fusion = bf16[32,32,1024]{2,1,0:T(8,128)(2,1)} fusion(bf16[32,256,1024]{2,1,0:T(8,128)(2,1)} %param.7, s32[32]{0:T(128)S(1)} %broadcast_subtract_fusion), kind=kOutput, calls=%fused_computation.7 | convolution fusion | flops 537927680 | bytes 18874496 | tf_op jit(solution)/shard_map/pj,bju->bpu/dot_general | solution.py:39
  17.3 34.6 %reduce-scatter.2.cloned.1.call-done = bf16[32,16,1024]{2,1,0:T(8,128)(2,1)} async-done(((bf16[32,32,1024]{2,1,0:T(8,128)(2,1)}), bf16[32,16,1024]{2,1,0:T(8,128)(2,1)}) %reduce-scatter.2.cloned.1.call-update) | async-done | bytes 1048592 | tf_op jit(solution)/shard_map/reduce_scatter | solution.py:40
  51.9 3.1 %fusion.7 = f32[32,16,128]{2,1,0:T(8,128)S(1)} fusion(bf16[32,512,128]{2,1,0:T(8,128)(2,1)} %param.10, bf16[32,16,1024]{2,1,0:T(8,128)(2,1)} %reduce-scatter.2.cloned.1.call-done), kind=kOutput, calls=%fused_computation.9 | convolution fusion | flops 67108864 | bytes 4980736 | tf_op jit(solution)/shard_map/brn,bnk->brk/dot_general | solution.py:23
  55.5 1.7 fusion.9
  59.0 40.8 %all-gather.2.cloned.1.call-done = bf16[512,16,128]{2,1,0:T(8,128)(2,1)} async-done(((bf16[32,16,128]{2,1,0:T(8,128)(2,1)}), bf16[512,16,128]{2,1,0:T(8,128)(2,1)}) %all-gather.2.cloned.1.call-update) | async-done | bytes 2097168 | tf_op jit(solution)/shard_map/all_gather | solution.py:44
  99.8 2.1 %fusion.4 = bf16[32,16,128]{2,0,1:T(8,128)(2,1)S(1)} fusion(bf16[512,16,128]{2,1,0:T(8,128)(2,1)} %all-gather.2.cloned.1.call-done, s32[32]{0:T(128)S(1)} %dynamic_slice.3), kind=kOutput, calls=%fused_computation.8 | convolution fusion | flops 67190784 | bytes 2228352 | tf_op jit(solution)/shard_map/sn,nrk->srk/dot_general | solution.py:47
  102.8 1.4 fusion.75
  109.0 1.4 fusion.67
  111.6 1.4 fusion.71
  115.2 1.4 fusion.59
  117.8 1.4 fusion.63
  121.3 1.4 fusion.51
  124.0 1.4 fusion.55
  127.6 1.5 fusion.43
  130.4 1.4 fusion.47
  135.1 2.0 %fusion.35 = f32[32,16,128]{2,1,0:T(8,128)S(1)} fusion(bf16[9,32,64,128]{3,2,1,0:T(8,128)(2,1)} %param.12, bf16[32,16,128]{2,1,0:T(8,128)(2,1)S(1)} %collective-permute-done), kind=kOutput, calls=%fused_computation.37 | convolution fusion | flops 8388608 | bytes 917504 | tf_op jit(solution)/shard_map/brn,bnk->brk/dot_general | solution.py:23
  140.3 4.3 %collective-permute-done.1 = bf16[32,16,128]{2,1,0:T(8,128)(2,1)S(1)} collective-permute-done((bf16[32,16,128]{2,1,0:T(8,128)(2,1)S(1)}, bf16[32,16,128]{2,1,0:T(8,128)(2,1)S(1)}, u32[]{:S(2)}, u32[]{:S(2)}) %collective-permute-start.1) | collective-permute-done | bytes 131104 | tf_op jit(solution)/shard_map/ppermute | solution.py:14
  144.6 1.4 fusion.27
  148.1 3.7 %collective-permute-done.2 = bf16[32,16,128]{2,1,0:T(8,128)(2,1)S(1)} collective-permute-done((bf16[32,16,128]{2,1,0:T(8,128)(2,1)S(1)}, bf16[32,16,128]{2,1,0:T(8,128)(2,1)S(1)}, u32[]{:S(2)}, u32[]{:S(2)}) %collective-permute-start.2) | collective-permute-done | bytes 131104 | tf_op jit(solution)/shard_map/ppermute | solution.py:14
  154.4 5.8 %collective-permute-done.3 = bf16[32,16,128]{2,1,0:T(8,128)(2,1)S(1)} collective-permute-done((bf16[32,16,128]{2,1,0:T(8,128)(2,1)S(1)}, bf16[32,16,128]{2,1,0:T(8,128)(2,1)S(1)}, u32[]{:S(2)}, u32[]{:S(2)}) %collective-permute-start.3) | collective-permute-done | bytes 131104 | tf_op jit(solution)/shard_map/ppermute | solution.py:14
  161.5 2.4 %fusion.134 = f32[32,16,4096]{2,1,0:T(8,128)S(1)} fusion(bf16[32,64,4096]{2,1,0:T(8,128)(2,1)S(1)} %bitcast.126, bf16[32,16,128]{2,1,0:T(8,128)(2,1)S(1)} %fusion.133), kind=kOutput, calls=%fused_computation.187 | convolution fusion | flops 268435456 | bytes 25296896 | tf_op jit(solution)/shard_map/brn,bnk->brk/dot_general | solution.py:23
  163.8 4.5 %fusion.136 = f32[32,16,4096]{2,1,0:T(8,128)} fusion(bf16[32,64,4096]{2,1,0:T(8,128)(2,1)S(1)} %bitcast.126, bf16[32,16,128]{2,1,0:T(8,128)(2,1)S(1)} %fusion.133), kind=kOutput, calls=%fused_computation.189 | convolution fusion | flops 268435456 | bytes 25296896 | tf_op jit(solution)/shard_map/brn,bnk->brk/dot_general | solution.py:20
  168.3 4.1 %fusion.1 = (bf16[32,16,2048]{2,1,0:T(8,128)(2,1)S(1)}, bf16[32,16,2048]{2,1,0:T(8,128)(2,1)S(1)}) fusion(f32[32,16,4096]{2,1,0:T(8,128)S(1)} %fusion.134, f32[32,16,4096]{2,1,0:T(8,128)} %fusion.136), kind=kLoop, calls=%fused_computation.3 | loop fusion | flops 4194304 | bytes 20971520 | tf_op jit(solution)/shard_map/convert
  172.5 2.5 %pad_maximum_fusion = bf16[32,16,4096]{2,1,0:T(8,128)(2,1)} fusion(bf16[32,16,2048]{2,1,0:T(8,128)(2,1)S(1)} %get-tuple-element.6, bf16[32,16,2048]{2,1,0:T(8,128)(2,1)S(1)} %get-tuple-element.5), kind=kLoop, calls=%fused_computation.4 | loop fusion | flops 8388608 | bytes 8388608 | tf_op jit(solution)/shard_map/concatenate | solution.py:26
  (96 shorter events, 32.5 us)
Async XLA Ops:
  6.5 45.4 %reduce-scatter.2.cloned.1.call-start = ((), (), s32[]{:S(2)}) async-start(), calls=%async_computation.1 | async-start | bytes 3145728 | tf_op jit(solution)/shard_map/reduce_scatter | solution.py:40
  17.3 82.6 %all-gather.2.cloned.1.call-start = ((), (), s32[]{:S(2)}) async-start(), calls=%async_computation.2 | async-start | bytes 2228224 | tf_op jit(solution)/shard_map/all_gather | solution.py:44
  51.9 3.6 %copy-start = (bf16[32,512,128]{2,1,0:T(8,128)(2,1)S(1)}, bf16[32,512,128]{2,1,0:T(8,128)(2,1)}, u32[]{:S(2)}) copy-start(bf16[32,512,128]{2,1,0:T(8,128)(2,1)} %param.10) | copy-start | bytes 12582916
  125.4 8.7 %slice-start.4 = ((s8[4718592]{0:T(1024)(128)(4,1)}), s8[524288]{0:T(1024)(128)(4,1)S(1)}, s32[]{:S(2)}) async-start(s8[4718592]{0:T(1024)(128)(4,1)} %bitcast.127), calls=%async_computation.7 | async-start | bytes 1048576
  127.6 6.5 %slice-start.5 = ((s8[4718592]{0:T(1024)(128)(4,1)}), s8[4194304]{0:T(1024)(128)(4,1)S(1)}, s32[]{:S(2)}) async-start(s8[4718592]{0:T(1024)(128)(4,1)} %bitcast.127), calls=%async_computation.8 | async-start | bytes 8388608
  133.3 12.7 %slice-start.6 = ((s8[4718592]{0:T(1024)(128)(4,1)}), s8[4194304]{0:T(1024)(128)(4,1)S(1)}, s32[]{:S(2)}) async-start(s8[4718592]{0:T(1024)(128)(4,1)} %bitcast.129), calls=%async_computation.9 | async-start | bytes 8388608
  133.7 1.4 collective-permute-start
  134.0 27.4 %slice-start = ((s8[16777216]{0:T(1024)(128)(4,1)}), s8[4194304]{0:T(1024)(128)(4,1)S(1)}, s32[]{:S(2)}) async-start(s8[16777216]{0:T(1024)(128)(4,1)} %bitcast.125), calls=%async_computation.3 | async-start | bytes 8388608
  137.1 8.9 %slice-start.7 = ((s8[4718592]{0:T(1024)(128)(4,1)}), s8[524288]{0:T(1024)(128)(4,1)S(1)}, s32[]{:S(2)}) async-start(s8[4718592]{0:T(1024)(128)(4,1)} %bitcast.129), calls=%async_computation.10 | async-start | bytes 1048576
  138.9 22.5 %slice-start.1 = ((s8[16777216]{0:T(1024)(128)(4,1)}), s8[4194304]{0:T(1024)(128)(4,1)S(1)}, s32[]{:S(2)}) async-start(s8[16777216]{0:T(1024)(128)(4,1)} %bitcast.125), calls=%async_computation.4 | async-start | bytes 8388608
  138.9 5.7 %collective-permute-start.1 = (bf16[32,16,128]{2,1,0:T(8,128)(2,1)S(1)}, bf16[32,16,128]{2,1,0:T(8,128)(2,1)S(1)}, u32[]{:S(2)}, u32[]{:S(2)}) collective-permute-start(bf16[32,16,128]{2,1,0:T(8,128)(2,1)S(1)} %fusion.130), channel_id=1, source_target_pairs={{0,4},{4,0},{2,6},{6,2},{8,12},{12,8},{10,14},{14,10},{16,20},{20,... | collective-permute-start | bytes 393224 | tf_op jit(solution)/shard_map/ppermute | solution.py:14
  146.7 14.7 %slice-start.2 = ((s8[16777216]{0:T(1024)(128)(4,1)}), s8[4194304]{0:T(1024)(128)(4,1)S(1)}, s32[]{:S(2)}) async-start(s8[16777216]{0:T(1024)(128)(4,1)} %bitcast.125), calls=%async_computation.5 | async-start | bytes 8388608
  146.7 5.0 %collective-permute-start.2 = (bf16[32,16,128]{2,1,0:T(8,128)(2,1)S(1)}, bf16[32,16,128]{2,1,0:T(8,128)(2,1)S(1)}, u32[]{:S(2)}, u32[]{:S(2)}) collective-permute-start(bf16[32,16,128]{2,1,0:T(8,128)(2,1)S(1)} %fusion.131), channel_id=1, source_target_pairs={{0,8},{8,0},{2,10},{10,2},{4,12},{12,4},{6,14},{14,6},{16,24},{24,... | collective-permute-start | bytes 393224 | tf_op jit(solution)/shard_map/ppermute | solution.py:14
  152.8 8.7 %slice-start.3 = ((s8[16777216]{0:T(1024)(128)(4,1)}), s8[4194304]{0:T(1024)(128)(4,1)S(1)}, s32[]{:S(2)}) async-start(s8[16777216]{0:T(1024)(128)(4,1)} %bitcast.125), calls=%async_computation.6 | async-start | bytes 8388608
  152.8 7.4 %collective-permute-start.3 = (bf16[32,16,128]{2,1,0:T(8,128)(2,1)S(1)}, bf16[32,16,128]{2,1,0:T(8,128)(2,1)S(1)}, u32[]{:S(2)}, u32[]{:S(2)}) collective-permute-start(bf16[32,16,128]{2,1,0:T(8,128)(2,1)S(1)} %fusion.132), channel_id=1, source_target_pairs={{0,16},{16,0},{2,18},{18,2},{4,20},{20,4},{6,22},{22,6},{8,24},{24... | collective-permute-start | bytes 393224 | tf_op jit(solution)/shard_map/ppermute | solution.py:14
Sparse Core Ops, SparseCore 0:
  17.4 34.4 reduce-scatter.1
  58.4 41.3 all-gather.1
where the time goes:
time: 183 us; the launch traced here: 182 us
  waiting for transfers between devices  89.5 us (49%)
  matrix products  58.8 us (32%)
  other arithmetic  14.9 us (8%)
  between operations  13.9 us (8%)
  starting transfers between devices  2.44 us (1%)
  local copies, waits for them, and re-layouts  2.31 us (1%)
    all_gather x1, waiting for transfers between devices, per_device(): piece = lax.all_gather(coefs, 'box', axis=0, tiled=True)  40.8 us
    reduce_scatter x1, waiting for transfers between devices, per_device(): lax.psum_scatter(picked.astype(jnp.bfloat16), 'tx', scatter_dimension=1,...  34.6 us
    dot_general x20, matrix products, complex_times(): jnp.einsum('brn,bnk->brk', values[..., inner:], matrix, preferred_element...  24.4 us
    dot_general x20, matrix products, complex_times(): jnp.einsum('brn,bnk->brk', values[..., :inner], matrix, preferred_element...  22.2 us
    ppermute x4, waiting for transfers between devices, partner_2(): return lax.ppermute(block, axis, route)  14 us
    dot_general x1, matrix products, per_device(): jnp.einsum('pj,bju->bpu', chooser, bank, preferred_element_type=jnp.float32)  10.1 us
    another operation x2, other arithmetic  4.34 us
    sub x17, other arithmetic, complex_times(): first[..., :half] - second[..., half:]  3.96 us
  transfers between devices with their start and end apart: 6, of which 6 were waited for; matrix products, arithmetic and copies ran while one was open for 2% of the time, Pallas kernels for 0%

commit v1 on v0

v1 whole, which is shorter than its diff:
```python
import functools

import jax
import jax.numpy as jnp
from jax import lax
from jax.experimental import pallas as pl
from jax.experimental.pallas import tpu as pltpu
from jax.sharding import PartitionSpec as P

BF16 = jnp.bfloat16
F32 = jnp.float32
MIB = 1 << 20
BATCH = 4


def dot(a, b):
    return jnp.dot(a, b, preferred_element_type=F32)


def lanes_below(shape, bound):
    return lax.broadcasted_iota(jnp.int32, shape, len(shape) - 1) < bound


def combine(first, second, rank):
    turned = pltpu.roll(second, rank, 1)
    return first + jnp.where(lanes_below(turned.shape, rank), -turned, turned)


def stack_pair(own, other, rank):
    low = lanes_below(own.shape, rank)
    real = jnp.where(low, own, pltpu.roll(other, rank, 1))
    imag = jnp.where(low, pltpu.roll(own, rank, 1), other)
    return jnp.concatenate([real, imag], axis=0).astype(BF16)


def leaf_kernel(
    cols,
    pick_ref,
    slot_ref,
    bank_ref,
    leaf_ref,
    out_ref,
    perm_ref,
    bank,
    leaf,
    chooser,
    chosen,
    coefs,
    bank_sems,
    leaf_sems,
):
    box_dev, stored, unknowns = bank_ref.shape
    unknowns //= 2
    rank = leaf_ref.shape[-1] // 2
    picked = pick_ref.shape[0]

    def bank_copy(b):
        return pltpu.make_async_copy(bank_ref.at[b], bank.at[b], bank_sems.at[b])

    def leaf_copy(b):
        return pltpu.make_async_copy(leaf_ref.at[b], leaf.at[b], leaf_sems.at[b])

    def start(b, _):
        bank_copy(b).start()
        leaf_copy(b).start()
        return 0

    lax.fori_loop(0, box_dev, start, 0)

    base = lax.axis_index("tx") * stored
    row = lax.broadcasted_iota(jnp.int32, (picked, stored), 0)
    column = lax.broadcasted_iota(jnp.int32, (picked, stored), 1)
    wanted = jnp.full((picked, stored), -1, jnp.int32)
    for c in range(picked):
        wanted = jnp.where(row == c, pick_ref[c] - base, wanted)
    chooser[...] = (wanted == column).astype(F32).astype(BF16)
    count = slot_ref.shape[1]
    for c in range(0, count, 128):
        box = lax.broadcasted_iota(jnp.int32, (count, 128), 0)
        hit = (box == slot_ref[:, c : c + 128]).astype(F32)
        perm_ref[c : c + 128, :] = hit.T.astype(BF16)

    def select(g):
        for i in range(BATCH):
            bank_copy(g * BATCH + i).wait()
        for i in range(BATCH):
            rows = dot(chooser[...], bank[g * BATCH + i]).astype(BF16)
            chosen[g % 2, i] = jnp.concatenate([rows[:, :unknowns], rows[:, unknowns:]], axis=0)

    def map_leaves(g):
        for i in range(BATCH):
            leaf_copy(g * BATCH + i).wait()
        for i in range(BATCH):
            product = dot(chosen[g % 2, i], leaf[g * BATCH + i])
            place = pl.multiple_of((g * BATCH + i) * picked, picked)
            coefs[pl.ds(place, picked), :] = combine(product[:picked], product[picked:], rank)

    def advance(g, _):
        for i in range(BATCH):
            bank_copy(g * BATCH + i).wait()
            leaf_copy((g - 1) * BATCH + i).wait()
        for i in range(BATCH):
            rows = dot(chooser[...], bank[g * BATCH + i]).astype(BF16)
            chosen[g % 2, i] = jnp.concatenate([rows[:, :unknowns], rows[:, unknowns:]], axis=0)
            product = dot(chosen[(g - 1) % 2, i], leaf[(g - 1) * BATCH + i])
            place = pl.multiple_of(((g - 1) * BATCH + i) * picked, picked)
            coefs[pl.ds(place, picked), :] = combine(product[:picked], product[picked:], rank)
        return 0

    batches = box_dev // BATCH
    select(0)
    lax.fori_loop(1, batches, advance, 0)
    map_leaves(batches - 1)
    groups = picked // cols
    for c in range(picked):
        place = (c % cols) * groups + c // cols
        out_ref[place] = coefs[pl.ds(c, box_dev, stride=picked), :].astype(BF16)


def leaf_step(cols, bank, pick, slot_box, leaf_factor):
    box_dev, stored, width = bank.shape
    picked = pick.shape[0]
    count = slot_box.shape[0]
    rank2 = leaf_factor.shape[-1]
    return pl.pallas_call(
        functools.partial(leaf_kernel, cols),
        out_shape=(
            jax.ShapeDtypeStruct((picked, box_dev, rank2), BF16),
            jax.ShapeDtypeStruct((count, count), BF16),
        ),
        in_specs=[
            pl.BlockSpec(memory_space=pltpu.SMEM),
            pl.BlockSpec(memory_space=pltpu.VMEM),
            pl.BlockSpec(memory_space=pltpu.HBM),
            pl.BlockSpec(memory_space=pltpu.HBM),
        ],
        out_specs=(
            pl.BlockSpec(memory_space=pltpu.VMEM),
            pl.BlockSpec(memory_space=pltpu.VMEM),
        ),
        scratch_shapes=[
            pltpu.VMEM(bank.shape, BF16),
            pltpu.VMEM(leaf_factor.shape, BF16),
            pltpu.VMEM((picked, stored), BF16),
            pltpu.VMEM((2, BATCH, 2 * picked, width // 2), BF16),
            pltpu.VMEM((box_dev * picked, rank2), F32),
            pltpu.SemaphoreType.DMA((box_dev,)),
            pltpu.SemaphoreType.DMA((box_dev,)),
        ],
        compiler_params=pltpu.CompilerParams(vmem_limit_bytes=56 * MIB),
        name="select_and_leaf",
    )(pick, slot_box.reshape(1, count), bank, leaf_factor)


def order_kernel(perm_ref, sent_ref, out_ref):
    devices, groups, box_dev, width = sent_ref.shape
    total = sent_ref[:, 0].astype(F32)
    for t in range(1, groups):
        total = total + sent_ref[:, t].astype(F32)
    rows = total.reshape(devices * box_dev, width).astype(BF16)
    out_ref[...] = dot(perm_ref[...], rows).astype(BF16).reshape(out_ref.shape)


def order_step(perm, sent):
    devices, _, box_dev, width = sent.shape
    return pl.pallas_call(
        order_kernel,
        out_shape=jax.ShapeDtypeStruct((devices, box_dev, width), BF16),
        in_specs=[pl.BlockSpec(memory_space=pltpu.VMEM)] * 2,
        out_specs=pl.BlockSpec(memory_space=pltpu.VMEM),
        compiler_params=pltpu.CompilerParams(vmem_limit_bytes=8 * MIB),
        name="leaf_order",
    )(perm, sent)


def local_kernel(local_bits, leaves_ref, self_ref, cross_ref, out_ref, wide, state):
    cols, slots, rank2 = leaves_ref.shape
    rank = rank2 // 2
    wide[...] = leaves_ref[...].astype(F32).reshape(cols * slots, rank2)
    for s in range(slots):
        state[0, s] = wide[pl.ds(s, cols, stride=slots), :]
    for level in range(local_bits):
        span = 1 << level
        now, later = level % 2, (level + 1) % 2
        for s in range(slots):
            if s & span:
                continue
            p = s | span
            left = jnp.concatenate([self_ref[level, s], cross_ref[level, s]], axis=0)
            right = jnp.concatenate([cross_ref[level, p], self_ref[level, p]], axis=0)
            both = dot(
                stack_pair(state[now, s], state[now, p], rank),
                jnp.concatenate([left, right], axis=1),
            )
            for place, product in ((s, both[:, :rank2]), (p, both[:, rank2:])):
                mixed = combine(product[:cols], product[cols:], rank)
                if level == local_bits - 1:
                    out_ref[place] = mixed.astype(BF16)
                else:
                    state[later, place] = mixed


def local_step(local_bits, leaves, self_factor, cross_factor):
    cols, slots, rank2 = leaves.shape
    return pl.pallas_call(
        functools.partial(local_kernel, local_bits),
        out_shape=jax.ShapeDtypeStruct((slots, cols, rank2), BF16),
        in_specs=[pl.BlockSpec(memory_space=pltpu.VMEM)] * 3,
        out_specs=pl.BlockSpec(memory_space=pltpu.VMEM),
        scratch_shapes=[
            pltpu.VMEM((cols * slots, rank2), F32),
            pltpu.VMEM((2, slots, cols, rank2), F32),
        ],
        compiler_params=pltpu.CompilerParams(vmem_limit_bytes=16 * MIB),
        name="local_levels",
    )(leaves, self_factor, cross_factor)


def mix_slot(level, s, own_ref, other_ref, self_ref, cross_ref):
    cols, rank2 = own_ref.shape[1:]
    rank = rank2 // 2
    rows = stack_pair(own_ref[s].astype(F32), other_ref[s].astype(F32), rank)
    product = dot(rows, jnp.concatenate([self_ref[level, s], cross_ref[level, s]], axis=0))
    return combine(product[:cols], product[cols:], rank)


def pair_kernel(level, own_ref, other_ref, self_ref, cross_ref, out_ref):
    for s in range(own_ref.shape[0]):
        out_ref[s] = mix_slot(level, s, own_ref, other_ref, self_ref, cross_ref).astype(BF16)


def pair_step(level, own, other, self_factor, cross_factor):
    return pl.pallas_call(
        functools.partial(pair_kernel, level),
        out_shape=jax.ShapeDtypeStruct(own.shape, BF16),
        in_specs=[pl.BlockSpec(memory_space=pltpu.VMEM)] * 4,
        out_specs=pl.BlockSpec(memory_space=pltpu.VMEM),
        compiler_params=pltpu.CompilerParams(vmem_limit_bytes=16 * MIB),
        name="pair_level",
    )(own, other, self_factor, cross_factor)


GROUP = 4
TILE = 512


def field_kernel(
    level, own_ref, other_ref, self_ref, cross_ref, target_ref, out_ref, final, result, sems
):
    slots, cols, rank2 = own_ref.shape
    rank = rank2 // 2
    points = target_ref.shape[-1] // 2
    for s in range(slots):
        final[s] = mix_slot(level, s, own_ref, other_ref, self_ref, cross_ref)

    def out_copy(q):
        part = pl.ds(q * GROUP, GROUP)
        return pltpu.make_async_copy(result.at[part], out_ref.at[part], sems.at[q])

    def group(q, _):
        rows = []
        for i in range(GROUP):
            values = final[q * GROUP + i]
            turned = pltpu.roll(values, rank, 1)
            low = lanes_below(values.shape, rank)
            real, imag = (values, turned) if i % 2 == 0 else (turned, values)
            keep = low if i % 2 == 0 else jnp.logical_not(low)
            block = jnp.concatenate([jnp.where(keep, real, 0.0), jnp.where(keep, imag, 0.0)], axis=0)
            empty = jnp.zeros_like(block)
            rows.append(
                jnp.concatenate([block if j == i // 2 else empty for j in range(GROUP // 2)], axis=1)
            )
        rows = jnp.concatenate(rows, axis=0).astype(BF16)
        part = pl.ds(q * GROUP, GROUP)
        for start in range(0, points, TILE):
            real_part = target_ref[part, :, pl.ds(start, TILE)].reshape(GROUP * rank, TILE)
            imag_part = target_ref[part, :, pl.ds(points + start, TILE)].reshape(GROUP * rank, TILE)
            by_real = dot(rows, real_part)
            by_imag = dot(rows, imag_part)
            for i in range(GROUP):
                xr = slice(2 * cols * i, 2 * cols * i + cols)
                xi = slice(2 * cols * i + cols, 2 * cols * (i + 1))
                box = q * GROUP + i
                result[box, :, pl.ds(start, TILE)] = (by_real[xr] - by_imag[xi]).astype(BF16)
                result[box, :, pl.ds(points + start, TILE)] = (by_imag[xr] + by_real[xi]).astype(BF16)
        out_copy(q).start()
        return 0

    lax.fori_loop(0, slots // GROUP, group, 0)
    for q in range(slots // GROUP):
        out_copy(q).wait()


def field_step(level, own, other, self_factor, cross_factor, target_factor):
    slots, cols, rank2 = own.shape
    width = target_factor.shape[-1]
    return pl.pallas_call(
        functools.partial(field_kernel, level),
        out_shape=jax.ShapeDtypeStruct((slots, cols, width), BF16),
        in_specs=[pl.BlockSpec(memory_space=pltpu.VMEM)] * 5,
        out_specs=pl.BlockSpec(memory_space=pl.ANY),
        scratch_shapes=[
            pltpu.VMEM((slots, cols, rank2), F32),
            pltpu.VMEM((slots, cols, width), BF16),
            pltpu.SemaphoreType.DMA((slots // GROUP,)),
        ],
        compiler_params=pltpu.CompilerParams(vmem_limit_bytes=22 * MIB),
        name="last_level_and_field",
    )(own, other, self_factor, cross_factor, target_factor)


def per_device(bank, pick, slot_box, leaf_factor, self_factor, cross_factor, target_factor):
    box_dev = bank.shape[0]
    devices = lax.axis_size("box")
    groups = lax.axis_size("tx")
    cols = pick.shape[0] // groups
    rank2 = leaf_factor.shape[-1]
    levels = self_factor.shape[0]
    local_bits = box_dev.bit_length() - 1
    parts = devices // cols
    width = rank2 // parts

    sent, perm = leaf_step(cols, bank, pick, slot_box, leaf_factor)
    if parts > 1:
        sent = sent.reshape(cols, groups, box_dev, parts, width).transpose(0, 3, 1, 2, 4)
        sent = sent.reshape(devices * groups, box_dev, width)
    sent = lax.all_to_all(sent, ("box", "tx"), 0, 0, tiled=True)
    ordered = order_step(perm, sent.reshape(devices, groups, box_dev, width))
    leaves = lax.all_to_all(ordered, "box", 0, 0, tiled=True)
    if parts > 1:
        leaves = leaves.reshape(cols, parts, box_dev, width).transpose(0, 2, 1, 3)
        leaves = leaves.reshape(cols, box_dev, rank2)
    current = local_step(local_bits, leaves, self_factor, cross_factor)
    for level in range(local_bits, levels):
        bit = 1 << (level - local_bits)
        other = lax.ppermute(current, "box", [(i, i ^ bit) for i in range(devices)])
        if level < levels - 1:
            current = pair_step(level, current, other, self_factor, cross_factor)
    return field_step(level, current, other, self_factor, cross_factor, target_factor)


def solution(mesh):
    in_specs = (
        P("box", "tx", None),
        P(),
        P(),
        P("box", None, None),
        P(None, "box", None, None),
        P(None, "box", None, None),
        P("box", None, None),
    )
    out_specs = P("box", "tx", None)
    return jax.shard_map(
        per_device, mesh=mesh, in_specs=in_specs, out_specs=out_specs, check_vma=False
    )
```

time: 183 us -> 72.4 us (0.40)
  waiting for transfers between devices: 89.5 us -> 18.5 us
  matrix products: 58.8 us -> 0 us
  blocking collectives: 0 us -> 28.5 us
  Pallas kernels: 0 us -> 21 us
  other arithmetic: 14.9 us -> 0.01 us
  between operations: 13.9 us -> 0.08 us
  starting transfers between devices: 2.44 us -> 0.6 us
    dot_general x42 -> x0, matrix products: 58.8 us -> none  [the longest x20 24.4 us: complex_times(): jnp.einsum('brn,bnk->brk', values[..., inner:], matrix, preferred_element...]
    all_gather x1 -> x0, waiting for transfers between devices: 40.8 us -> none  [per_device(): piece = lax.all_gather(coefs, 'box', axis=0, tiled=True)]
    reduce_scatter x1 -> x0, waiting for transfers between devices: 34.6 us -> none  [per_device(): lax.psum_scatter(picked.astype(jnp.bfloat16), 'tx', scatter_dimension=1,...]
    all_to_all x0 -> x2, blocking collectives: none -> 28.5 us  [the longest x1 18 us: per_device(): sent = lax.all_to_all(sent, ('box', 'tx'), 0, 0, tiled=True)]
    pallas_call x0 -> x7, Pallas kernels: none -> 21 us  [the longest x1 12 us: leaf_step(): pl.pallas_call(functools.partial(leaf_kernel, cols), out_shape=(jax.Shape...]
    sub x18 -> x0, other arithmetic: 4.61 us -> none  [the longest x17 3.96 us: complex_times(): first[..., :half] - second[..., half:]]
    ppermute x4, waiting for transfers between devices: 14 us -> 18.5 us  [per_device(): other = lax.ppermute(current, 'box', [(i, i ^ bit) for i in range(devices)])]
    another operation x2 -> x0, other arithmetic: 4.34 us -> none
  transfers between devices with their start and end apart: 6 -> 4, of which waited for: 6 -> 4; matrix products, arithmetic and copies ran while one was open for 2% -> 0% of each run, Pallas kernels for 0% -> 0%
where the time goes in v1:
time: 72.4 us; the launch traced here: 72.1 us
  blocking collectives  28.5 us (39%)
  Pallas kernels  21 us (29%)
  waiting for transfers between devices  18.5 us (26%)
  local copies, waits for them, and re-layouts  3.4 us (5%)
    ppermute x4, waiting for transfers between devices, per_device(): other = lax.ppermute(current, 'box', [(i, i ^ bit) for i in range(devices)])  18.5 us
    all_to_all x1, blocking collectives, per_device(): sent = lax.all_to_all(sent, ('box', 'tx'), 0, 0, tiled=True)  18 us
    pallas_call x1, Pallas kernels, leaf_step(): pl.pallas_call(functools.partial(leaf_kernel, cols), out_shape=(jax.Shape...  12 us
    all_to_all x1, blocking collectives, per_device(): leaves = lax.all_to_all(ordered, 'box', 0, 0, tiled=True)  10.5 us
    pallas_call x1, Pallas kernels, field_step(): pl.pallas_call(functools.partial(field_kernel, level), out_shape=jax.Shap...  5.29 us
    unnamed x12, local copies, waits for them, and re-layouts  3.4 us
    pallas_call x1, Pallas kernels, local_step(): pl.pallas_call(functools.partial(local_kernel, local_bits), out_shape=jax...  1.87 us
    pallas_call x3, Pallas kernels, pair_step(): pl.pallas_call(functools.partial(pair_kernel, level), out_shape=jax.Shape...  1.53 us
  transfers between devices with their start and end apart: 4, of which 4 were waited for; matrix products, arithmetic and copies ran while one was open for 0% of the time, Pallas kernels for 0%

profile of v1, /device:TPU:0, one launch (start us, length us, event | category | flops | bytes accessed | tf_op | source)
XLA Modules:
  0.0 72.1 jit_solution(14529538253435789734)
XLA Ops:
  0.0 12.0 %select_and_leaf.1 = (bf16[32,32,128]{2,1,0:T(8,128)(2,1)}, bf16[512,512]{1,0:T(8,128)(2,1)}) custom-call(s32[32]{0:T(128)} %pick_ref.1, s32[1,512]{1,0:T(1,128)} %bitcast.5, bf16[32,256,1024]{2,1,0:T(8,128)(2,1)} %bank_ref.1, bf16[32,512,128]{2,1,0:T(8,128)(2,1)} %leaf_ref.1), custom_call_target="tpu_custom_call" | custom-call | tf_op jit(solution)/shard_map/select_and_leaf/pallas_call | solution.py:125
  12.0 18.0 %all_to_all.10 = bf16[32,32,128]{2,1,0:T(8,128)(2,1)S(1)} all-to-all(bf16[32,32,128]{2,1,0:T(8,128)(2,1)} %get-tuple-element.8), channel_id=1, replica_groups=mesh['box'=16,'tx'=2] {'box','tx'}, dimensions={0} | all-to-all | bytes 524288 | tf_op jit(solution)/shard_map/all_to_all | solution.py:327
  30.0 1.0 %copy-done.3 = bf16[512,512]{1,0:T(8,128)(2,1)S(1)} copy-done((bf16[512,512]{1,0:T(8,128)(2,1)S(1)}, bf16[512,512]{1,0:T(8,128)(2,1)}, u32[]{:S(2)}) %copy-start.3) | copy-done | bytes 524312
  31.0 0.3 leaf_order.1
  31.3 10.5 %all_to_all.11.leaves_ref = bf16[16,32,128]{2,1,0:T(8,128)(2,1)S(1)} all-to-all(bf16[16,32,128]{2,1,0:T(8,128)(2,1)S(1)} %leaf_order.1), channel_id=1, replica_groups=mesh['box'=16,'tx'=2] {'box'}, dimensions={0} | all-to-all | bytes 262144 | tf_op jit(solution)/shard_map/all_to_all | solution.py:329
  41.9 0.0 copy-done
  41.9 2.3 %copy-done.1 = bf16[9,32,64,128]{3,2,1,0:T(8,128)(2,1)S(1)} copy-done((bf16[9,32,64,128]{3,2,1,0:T(8,128)(2,1)S(1)}, bf16[9,32,64,128]{3,2,1,0:T(8,128)(2,1)}, u32[]{:S(2)}) %copy-start.1) | copy-done | bytes 4718616
  44.2 1.9 %local_levels.1.own_ref = bf16[32,16,128]{2,1,0:T(8,128)(2,1)S(1)} custom-call(bf16[16,32,128]{2,1,0:T(8,128)(2,1)S(1)} %all_to_all.11.leaves_ref, bf16[9,32,64,128]{3,2,1,0:T(8,128)(2,1)S(1)} %copy-done, bf16[9,32,64,128]{3,2,1,0:T(8,128)(2,1)S(1)} %copy-done.1), custom_call_target="tpu_custom_call" | custom-call | tf_op jit(solution)/shard_map/local_levels/pallas_call | solution.py:205
  46.1 0.1 collective-permute-start
  46.2 1.3 %collective-permute-done.other_ref = bf16[32,16,128]{2,1,0:T(8,128)(2,1)S(1)} collective-permute-done((bf16[32,16,128]{2,1,0:T(8,128)(2,1)S(1)}, bf16[32,16,128]{2,1,0:T(8,128)(2,1)S(1)}, u32[]{:S(2)}, u32[]{:S(2)}) %collective-permute-start) | collective-permute-done | bytes 131104 | tf_op jit(solution)/shard_map/ppermute | solution.py:336
  47.5 0.5 pair_level.3.own_ref
  48.0 0.1 collective-permute-start.1
  48.1 5.5 %collective-permute-done.1.other_ref = bf16[32,16,128]{2,1,0:T(8,128)(2,1)S(1)} collective-permute-done((bf16[32,16,128]{2,1,0:T(8,128)(2,1)S(1)}, bf16[32,16,128]{2,1,0:T(8,128)(2,1)S(1)}, u32[]{:S(2)}, u32[]{:S(2)}) %collective-permute-start.1) | collective-permute-done | bytes 131104 | tf_op jit(solution)/shard_map/ppermute | solution.py:336
  53.6 0.5 pair_level.4.own_ref
  54.1 0.0 slice-start.1
  54.2 0.1 collective-permute-start.2
  54.2 5.0 %collective-permute-done.2.other_ref = bf16[32,16,128]{2,1,0:T(8,128)(2,1)S(1)} collective-permute-done((bf16[32,16,128]{2,1,0:T(8,128)(2,1)S(1)}, bf16[32,16,128]{2,1,0:T(8,128)(2,1)S(1)}, u32[]{:S(2)}, u32[]{:S(2)}) %collective-permute-start.2) | collective-permute-done | bytes 131104 | tf_op jit(solution)/shard_map/ppermute | solution.py:336
  59.2 0.5 pair_level.5.own_ref
  59.7 0.4 collective-permute-start.3
  60.1 6.7 %collective-permute-done.3.other_ref = bf16[32,16,128]{2,1,0:T(8,128)(2,1)S(1)} collective-permute-done((bf16[32,16,128]{2,1,0:T(8,128)(2,1)S(1)}, bf16[32,16,128]{2,1,0:T(8,128)(2,1)S(1)}, u32[]{:S(2)}, u32[]{:S(2)}) %collective-permute-start.3) | collective-permute-done | bytes 131104 | tf_op jit(solution)/shard_map/ppermute | solution.py:336
  66.8 0.0 copy-done.2
  66.8 0.0 slice-done
  66.8 0.0 slice-done.1
  66.8 5.3 %last_level_and_field.1 = bf16[32,16,4096]{2,1,0:T(8,128)(2,1)} custom-call(bf16[32,16,128]{2,1,0:T(8,128)(2,1)S(1)} %pair_level.5.own_ref, bf16[32,16,128]{2,1,0:T(8,128)(2,1)S(1)} %collective-permute-done.3.other_ref, bf16[9,32,64,128]{3,2,1,0:T(8,128)(2,1)S(1)} %copy-done, bf16[9,32,64,128]{3,2,1,0:T(8,128)(2,1)S(1)} %bitcast.3, ...), custom_call_target="tpu_custom_call" | custom-call | tf_op jit(solution)/shard_map/last_level_and_field/pallas_call | solution.py:297
  (6 shorter events, 0.0 us)
Async XLA Ops:
  0.0 41.9 %copy-start = (bf16[9,32,64,128]{3,2,1,0:T(8,128)(2,1)S(1)}, bf16[9,32,64,128]{3,2,1,0:T(8,128)(2,1)}, u32[]{:S(2)}) copy-start(bf16[9,32,64,128]{3,2,1,0:T(8,128)(2,1)} %self_ref.9) | copy-start | bytes 14155780
  30.0 1.0 %copy-start.3 = (bf16[512,512]{1,0:T(8,128)(2,1)S(1)}, bf16[512,512]{1,0:T(8,128)(2,1)}, u32[]{:S(2)}) copy-start(bf16[512,512]{1,0:T(8,128)(2,1)} %get-tuple-element.7.perm_ref) | copy-start | bytes 1572868
  41.9 2.3 %copy-start.1 = (bf16[9,32,64,128]{3,2,1,0:T(8,128)(2,1)S(1)}, bf16[9,32,64,128]{3,2,1,0:T(8,128)(2,1)}, u32[]{:S(2)}) copy-start(bf16[9,32,64,128]{3,2,1,0:T(8,128)(2,1)} %cross_ref.9) | copy-start | bytes 14155780
  46.1 1.4 %collective-permute-start = (bf16[32,16,128]{2,1,0:T(8,128)(2,1)S(1)}, bf16[32,16,128]{2,1,0:T(8,128)(2,1)S(1)}, u32[]{:S(2)}, u32[]{:S(2)}) collective-permute-start(bf16[32,16,128]{2,1,0:T(8,128)(2,1)S(1)} %local_levels.1.own_ref), channel_id=1, source_target_pairs={{0,2},{2,0},{4,6},{6,4},{8,10},{10,8},{12,14},{14,12},{16,18},{18,... | collective-permute-start | bytes 393224 | tf_op jit(solution)/shard_map/ppermute | solution.py:336
  47.5 19.3 %copy-start.2 = (bf16[32,64,4096]{2,1,0:T(8,128)(2,1)S(1)}, bf16[32,64,4096]{2,1,0:T(8,128)(2,1)}, u32[]{:S(2)}) copy-start(bf16[32,64,4096]{2,1,0:T(8,128)(2,1)} %target_ref.1) | copy-start | bytes 50331652
  48.0 5.6 %collective-permute-start.1 = (bf16[32,16,128]{2,1,0:T(8,128)(2,1)S(1)}, bf16[32,16,128]{2,1,0:T(8,128)(2,1)S(1)}, u32[]{:S(2)}, u32[]{:S(2)}) collective-permute-start(bf16[32,16,128]{2,1,0:T(8,128)(2,1)S(1)} %pair_level.3.own_ref), channel_id=1, source_target_pairs={{0,4},{2,6},{4,0},{6,2},{8,12},{10,14},{12,8},{14,10},{16,20},{18,... | collective-permute-start | bytes 393224 | tf_op jit(solution)/shard_map/ppermute | solution.py:336
  53.6 13.1 %slice-start = ((s8[4718592]{0:T(1024)(128)(4,1)}), s8[4194304]{0:T(1024)(128)(4,1)S(1)}, s32[]{:S(2)}) async-start(s8[4718592]{0:T(1024)(128)(4,1)} %bitcast.2), calls=%async_computation.2 | async-start | bytes 8388608
  54.1 12.6 %slice-start.1 = ((s8[4718592]{0:T(1024)(128)(4,1)}), s8[524288]{0:T(1024)(128)(4,1)S(1)}, s32[]{:S(2)}) async-start(s8[4718592]{0:T(1024)(128)(4,1)} %bitcast.2), calls=%async_computation.3 | async-start | bytes 1048576
  54.2 5.0 %collective-permute-start.2 = (bf16[32,16,128]{2,1,0:T(8,128)(2,1)S(1)}, bf16[32,16,128]{2,1,0:T(8,128)(2,1)S(1)}, u32[]{:S(2)}, u32[]{:S(2)}) collective-permute-start(bf16[32,16,128]{2,1,0:T(8,128)(2,1)S(1)} %pair_level.4.own_ref), channel_id=1, source_target_pairs={{0,8},{2,10},{4,12},{6,14},{8,0},{10,2},{12,4},{14,6},{16,24},{18,... | collective-permute-start | bytes 393224 | tf_op jit(solution)/shard_map/ppermute | solution.py:336
  59.7 7.1 %collective-permute-start.3 = (bf16[32,16,128]{2,1,0:T(8,128)(2,1)S(1)}, bf16[32,16,128]{2,1,0:T(8,128)(2,1)S(1)}, u32[]{:S(2)}, u32[]{:S(2)}) collective-permute-start(bf16[32,16,128]{2,1,0:T(8,128)(2,1)S(1)} %pair_level.5.own_ref), channel_id=1, source_target_pairs={{0,16},{2,18},{4,20},{6,22},{8,24},{10,26},{12,28},{14,30},{16,0},... | collective-permute-start | bytes 393224 | tf_op jit(solution)/shard_map/ppermute | solution.py:336

commit v2 on v1

--- a/solution.py
+++ b/solution.py
@@ -10,7 +10,10 @@
 BF16 = jnp.bfloat16
 F32 = jnp.float32
 MIB = 1 << 20
-BATCH = 4
+BATCH = 8
+UNROLL = 8
+ROWS = 16
+LEAF_VMEM = 48
 
 
 def dot(a, b):
@@ -35,17 +38,21 @@
 
 def leaf_kernel(
     cols,
-    pick_ref,
-    slot_ref,
+    pick_hbm,
+    slot_hbm,
     bank_ref,
     leaf_ref,
     out_ref,
     perm_ref,
+    pick_ref,
+    slot_ref,
     bank,
     leaf,
-    chooser,
-    chosen,
     coefs,
+    present,
+    wanted,
+    rank_of,
+    index_sems,
     bank_sems,
     leaf_sems,
 ):
@@ -53,84 +60,109 @@
     unknowns //= 2
     rank = leaf_ref.shape[-1] // 2
     picked = pick_ref.shape[0]
-
-    def bank_copy(b):
-        return pltpu.make_async_copy(bank_ref.at[b], bank.at[b], bank_sems.at[b])
-
-    def leaf_copy(b):
-        return pltpu.make_async_copy(leaf_ref.at[b], leaf.at[b], leaf_sems.at[b])
-
-    def start(b, _):
-        bank_copy(b).start()
-        leaf_copy(b).start()
+    base = lax.axis_index("tx") * stored
+    batches = box_dev // BATCH
+    row_groups = stored // ROWS
+
+    def leaf_copy(g):
+        part = pl.ds(g * BATCH, BATCH)
+        return pltpu.make_async_copy(leaf_ref.at[part], leaf.at[part], leaf_sems.at[g])
+
+    def bank_copy(g, j):
+        part = pl.ds(g * BATCH, BATCH)
+        source = pl.ds(pl.multiple_of(wanted[j] * ROWS, ROWS), ROWS)
+        target = pl.ds(pl.multiple_of(j * ROWS, ROWS), ROWS)
+        return pltpu.make_async_copy(
+            bank_ref.at[part, source], bank.at[part, target], bank_sems.at[g, j]
+        )
+
+    pick_copy = pltpu.make_async_copy(pick_hbm, pick_ref, index_sems.at[0])
+    slot_copy = pltpu.make_async_copy(slot_hbm, slot_ref, index_sems.at[1])
+    pick_copy.start()
+    slot_copy.start()
+    leaf_copy(0).start()
+    pick_copy.wait()
+    for k in range(row_groups):
+        present[k] = 0
+    for c in range(picked):
+        place = pick_ref[c] - base
+
+        @pl.when(jnp.logical_and(place >= 0, place < stored))
+        def _():
+            present[place // ROWS] = 1
+
+    count = jnp.int32(0)
+    for k in range(row_groups):
+        wanted[count] = k
+        rank_of[k] = count
+        count = count + present[k]
+
+    def start(g, _):
+        lax.fori_loop(0, count, lambda j, _: (bank_copy(g, j).start(), 0)[1], 0)
+
+        @pl.when(g > 0)
+        def _():
+            leaf_copy(g).start()
+
         return 0
 
-    lax.fori_loop(0, box_dev, start, 0)
-
-    base = lax.axis_index("tx") * stored
-    row = lax.broadcasted_iota(jnp.int32, (picked, stored), 0)
-    column = lax.broadcasted_iota(jnp.int32, (picked, stored), 1)
-    wanted = jnp.full((picked, stored), -1, jnp.int32)
-    for c in range(picked):
-        wanted = jnp.where(row == c, pick_ref[c] - base, wanted)
-    chooser[...] = (wanted == column).astype(F32).astype(BF16)
-    count = slot_ref.shape[1]
-    for c in range(0, count, 128):
-        box = lax.broadcasted_iota(jnp.int32, (count, 128), 0)
+    lax.fori_loop(0, batches, start, 0)
+
+    slot_copy.wait()
+    boxes = slot_ref.shape[1]
+    for c in range(0, boxes, 128):
+        box = lax.broadcasted_iota(jnp.int32, (boxes, 128), 0)
         hit = (box == slot_ref[:, c : c + 128]).astype(F32)
         perm_ref[c : c + 128, :] = hit.T.astype(BF16)
 
-    def select(g):
-        for i in range(BATCH):
-            bank_copy(g * BATCH + i).wait()
-        for i in range(BATCH):
-            rows = dot(chooser[...], bank[g * BATCH + i]).astype(BF16)
-            chosen[g % 2, i] = jnp.concatenate([rows[:, :unknowns], rows[:, unknowns:]], axis=0)
-
-    def map_leaves(g):
-        for i in range(BATCH):
-            leaf_copy(g * BATCH + i).wait()
-        for i in range(BATCH):
-            product = dot(chosen[g % 2, i], leaf[g * BATCH + i])
-            place = pl.multiple_of((g * BATCH + i) * picked, picked)
-            coefs[pl.ds(place, picked), :] = combine(product[:picked], product[picked:], rank)
-
-    def advance(g, _):
-        for i in range(BATCH):
-            bank_copy(g * BATCH + i).wait()
-            leaf_copy((g - 1) * BATCH + i).wait()
-        for i in range(BATCH):
-            rows = dot(chooser[...], bank[g * BATCH + i]).astype(BF16)
-            chosen[g % 2, i] = jnp.concatenate([rows[:, :unknowns], rows[:, unknowns:]], axis=0)
-            product = dot(chosen[(g - 1) % 2, i], leaf[(g - 1) * BATCH + i])
-            place = pl.multiple_of(((g - 1) * BATCH + i) * picked, picked)
-            coefs[pl.ds(place, picked), :] = combine(product[:picked], product[picked:], rank)
+    def map_batch(g, _):
+        leaf_copy(g).wait()
+        lax.fori_loop(0, count, lambda j, _: (bank_copy(g, j).wait(), 0)[1], 0)
+
+        def map_boxes(rows):
+            def step(k, _):
+                for i in range(UNROLL):
+                    b = g * BATCH + k * UNROLL + i
+                    first = dot(bank[b, :rows, :unknowns], leaf[b])
+                    second = dot(bank[b, :rows, unknowns:], leaf[b])
+                    place = pl.ds(pl.multiple_of(b * stored, stored), rows)
+                    coefs[place, :] = combine(first, second, rank)
+                return 0
+
+            lax.fori_loop(0, BATCH // UNROLL, step, 0)
+
+        quarter = row_groups // 4
+        for part in range(2, 5):
+            low = 0 if part == 2 else (part - 1) * quarter
+            fits = jnp.logical_and(count > low, count <= part * quarter)
+            pl.when(fits)(functools.partial(map_boxes, part * quarter * ROWS))
         return 0
 
-    batches = box_dev // BATCH
-    select(0)
-    lax.fori_loop(1, batches, advance, 0)
-    map_leaves(batches - 1)
+    lax.fori_loop(0, batches, map_batch, 0)
     groups = picked // cols
     for c in range(picked):
-        place = (c % cols) * groups + c // cols
-        out_ref[place] = coefs[pl.ds(c, box_dev, stride=picked), :].astype(BF16)
+        place = pick_ref[c] - base
+        held = jnp.logical_and(place >= 0, place < stored)
+        place = jnp.where(held, place, 0)
+        row = jnp.where(held, rank_of[place // ROWS] * ROWS + place % ROWS, 0)
+        rows = coefs[pl.ds(row, box_dev, stride=stored), :]
+        out_ref[(c % cols) * groups + c // cols] = jnp.where(held, rows, 0.0).astype(BF16)
 
 
 def leaf_step(cols, bank, pick, slot_box, leaf_factor):
-    box_dev, stored, width = bank.shape
+    box_dev, stored, _ = bank.shape
     picked = pick.shape[0]
-    count = slot_box.shape[0]
+    boxes = slot_box.shape[0]
     rank2 = leaf_factor.shape[-1]
     return pl.pallas_call(
         functools.partial(leaf_kernel, cols),
         out_shape=(
             jax.ShapeDtypeStruct((picked, box_dev, rank2), BF16),
-            jax.ShapeDtypeStruct((count, count), BF16),
+            jax.ShapeDtypeStruct((boxes, boxes), BF16),
         ),
         in_specs=[
-            pl.BlockSpec(memory_space=pltpu.SMEM),
-            pl.BlockSpec(memory_space=pltpu.VMEM),
+            pl.BlockSpec(memory_space=pltpu.HBM),
+            pl.BlockSpec(memory_space=pltpu.HBM),
             pl.BlockSpec(memory_space=pltpu.HBM),
             pl.BlockSpec(memory_space=pltpu.HBM),
         ],
@@ -139,17 +171,26 @@
             pl.BlockSpec(memory_space=pltpu.VMEM),
         ),
         scratch_shapes=[
+            pltpu.SMEM(pick.shape, jnp.int32),
+            pltpu.VMEM((1, boxes), jnp.int32),
             pltpu.VMEM(bank.shape, BF16),
             pltpu.VMEM(leaf_factor.shape, BF16),
-            pltpu.VMEM((picked, stored), BF16),
-            pltpu.VMEM((2, BATCH, 2 * picked, width // 2), BF16),
-            pltpu.VMEM((box_dev * picked, rank2), F32),
-            pltpu.SemaphoreType.DMA((box_dev,)),
-            pltpu.SemaphoreType.DMA((box_dev,)),
+            pltpu.VMEM((box_dev * stored, rank2), F32),
+            pltpu.SMEM((stored // ROWS,), jnp.int32),
+            pltpu.SMEM((stored // ROWS,), jnp.int32),
+            pltpu.SMEM((stored // ROWS,), jnp.int32),
+            pltpu.SemaphoreType.DMA((2,)),
+            pltpu.SemaphoreType.DMA((box_dev // BATCH, stored // ROWS)),
+            pltpu.SemaphoreType.DMA((box_dev // BATCH,)),
         ],
-        compiler_params=pltpu.CompilerParams(vmem_limit_bytes=56 * MIB),
+        compiler_params=pltpu.CompilerParams(vmem_limit_bytes=LEAF_VMEM * MIB),
         name="select_and_leaf",
-    )(pick, slot_box.reshape(1, count), bank, leaf_factor)
+    )(
+        pltpu.with_memory_space_constraint(pick, pltpu.HBM),
+        pltpu.with_memory_space_constraint(slot_box.reshape(1, boxes), pltpu.HBM),
+        pltpu.with_memory_space_constraint(bank, pltpu.HBM),
+        pltpu.with_memory_space_constraint(leaf_factor, pltpu.HBM),
+    )
 
 
 def order_kernel(perm_ref, sent_ref, out_ref):
@@ -257,7 +298,7 @@
         part = pl.ds(q * GROUP, GROUP)
         return pltpu.make_async_copy(result.at[part], out_ref.at[part], sems.at[q])
 
-    def group(q, _):
+    def group(q):
         rows = []
         for i in range(GROUP):
             values = final[q * GROUP + i]
@@ -284,9 +325,9 @@
                 result[box, :, pl.ds(start, TILE)] = (by_real[xr] - by_imag[xi]).astype(BF16)
                 result[box, :, pl.ds(points + start, TILE)] = (by_imag[xr] + by_real[xi]).astype(BF16)
         out_copy(q).start()
-        return 0
-
-    lax.fori_loop(0, slots // GROUP, group, 0)
+
+    for q in range(slots // GROUP):
+        group(q)
     for q in range(slots // GROUP):
         out_copy(q).wait()
 
@@ -306,7 +347,13 @@
         ],
         compiler_params=pltpu.CompilerParams(vmem_limit_bytes=22 * MIB),
         name="last_level_and_field",
-    )(own, other, self_factor, cross_factor, target_factor)
+    )(
+        own,
+        other,
+        self_factor,
+        cross_factor,
+        pltpu.with_memory_space_constraint(target_factor, pltpu.VMEM),
+    )
 
 
 def per_device(bank, pick, slot_box, leaf_factor, self_factor, cross_factor, target_factor):

time: 72.4 us -> 64.1 us (0.89)
  Pallas kernels: 21 us -> 16 us
  local copies, waits for them, and re-layouts: 3.4 us -> 0.03 us
    unnamed x12, local copies, waits for them, and re-layouts: 3.4 us -> 0.03 us
    pallas_call x1, Pallas kernels: 12 us -> 8.73 us  [leaf_step(): pl.pallas_call(functools.partial(leaf_kernel, cols), out_shape=(jax.Shape...]
    pallas_call x1, Pallas kernels: 5.29 us -> 3.56 us  [field_step(): pl.pallas_call(functools.partial(field_kernel, level), out_shape=jax.Shap...]
where the time goes in v2:
time: 64.1 us; the launch traced here: 64 us
  blocking collectives  28.8 us (45%)
  waiting for transfers between devices  18.5 us (29%)
  Pallas kernels  16 us (25%)
    ppermute x4, waiting for transfers between devices, per_device(): other = lax.ppermute(current, 'box', [(i, i ^ bit) for i in range(devices)])  18.5 us
    all_to_all x1, blocking collectives, per_device(): sent = lax.all_to_all(sent, ('box', 'tx'), 0, 0, tiled=True)  18.3 us
    all_to_all x1, blocking collectives, per_device(): leaves = lax.all_to_all(ordered, 'box', 0, 0, tiled=True)  10.5 us
    pallas_call x1, Pallas kernels, leaf_step(): pl.pallas_call(functools.partial(leaf_kernel, cols), out_shape=(jax.Shape...  8.73 us
    pallas_call x1, Pallas kernels, field_step(): pl.pallas_call(functools.partial(field_kernel, level), out_shape=jax.Shap...  3.56 us
    pallas_call x1, Pallas kernels, local_step(): pl.pallas_call(functools.partial(local_kernel, local_bits), out_shape=jax...  1.87 us
    pallas_call x3, Pallas kernels, pair_step(): pl.pallas_call(functools.partial(pair_kernel, level), out_shape=jax.Shape...  1.53 us
  transfers between devices with their start and end apart: 4, of which 4 were waited for; matrix products, arithmetic and copies ran while one was open for 0% of the time, Pallas kernels for 0%

profile of v2, /device:TPU:0, one launch (start us, length us, event | category | flops | bytes accessed | tf_op | source)
XLA Modules:
  0.0 64.0 jit_solution(16424978802000051563)
XLA Ops:
  0.0 8.7 %select_and_leaf.1 = (bf16[32,32,128]{2,1,0:T(8,128)(2,1)S(1)}, bf16[512,512]{1,0:T(8,128)(2,1)S(1)}) custom-call(s32[32]{0:T(128)} %pick_hbm.1, s32[1,512]{1,0:T(1,128)} %bitcast.5, bf16[32,256,1024]{2,1,0:T(8,128)(2,1)} %bank_ref.1, bf16[32,512,128]{2,1,0:T(8,128)(2,1)} %leaf_ref.1), custom_call_target="tpu_custom_call" | custom-call | tf_op jit(solution)/shard_map/select_and_leaf/pallas_call | solution.py:157
  8.7 18.3 %all_to_all.10 = bf16[32,32,128]{2,1,0:T(8,128)(2,1)S(1)} all-to-all(bf16[32,32,128]{2,1,0:T(8,128)(2,1)S(1)} %get-tuple-element.8), channel_id=1, replica_groups=mesh['box'=16,'tx'=2] {'box','tx'}, dimensions={0} | all-to-all | bytes 524288 | tf_op jit(solution)/shard_map/all_to_all | solution.py:374
  27.0 0.3 leaf_order.1
  27.3 10.5 %all_to_all.11.leaves_ref = bf16[16,32,128]{2,1,0:T(8,128)(2,1)S(1)} all-to-all(bf16[16,32,128]{2,1,0:T(8,128)(2,1)S(1)} %leaf_order.1), channel_id=1, replica_groups=mesh['box'=16,'tx'=2] {'box'}, dimensions={0} | all-to-all | bytes 262144 | tf_op jit(solution)/shard_map/all_to_all | solution.py:376
  37.9 0.0 copy-done
  37.9 0.0 copy-done.1
  37.9 1.9 %local_levels.1.own_ref = bf16[32,16,128]{2,1,0:T(8,128)(2,1)S(1)} custom-call(bf16[16,32,128]{2,1,0:T(8,128)(2,1)S(1)} %all_to_all.11.leaves_ref, bf16[9,32,64,128]{3,2,1,0:T(8,128)(2,1)S(1)} %copy-done, bf16[9,32,64,128]{3,2,1,0:T(8,128)(2,1)S(1)} %copy-done.1), custom_call_target="tpu_custom_call" | custom-call | tf_op jit(solution)/shard_map/local_levels/pallas_call | solution.py:246
  39.7 0.0 slice-start.1
  39.8 0.1 collective-permute-start
  39.8 1.3 %collective-permute-done.other_ref = bf16[32,16,128]{2,1,0:T(8,128)(2,1)S(1)} collective-permute-done((bf16[32,16,128]{2,1,0:T(8,128)(2,1)S(1)}, bf16[32,16,128]{2,1,0:T(8,128)(2,1)S(1)}, u32[]{:S(2)}, u32[]{:S(2)}) %collective-permute-start) | collective-permute-done | bytes 131104 | tf_op jit(solution)/shard_map/ppermute | solution.py:383
  41.2 0.5 pair_level.3.own_ref
  41.7 0.0 slice-start.2
  41.7 0.1 collective-permute-start.1
  41.8 5.5 %collective-permute-done.1.other_ref = bf16[32,16,128]{2,1,0:T(8,128)(2,1)S(1)} collective-permute-done((bf16[32,16,128]{2,1,0:T(8,128)(2,1)S(1)}, bf16[32,16,128]{2,1,0:T(8,128)(2,1)S(1)}, u32[]{:S(2)}, u32[]{:S(2)}) %collective-permute-start.1) | collective-permute-done | bytes 131104 | tf_op jit(solution)/shard_map/ppermute | solution.py:383
  47.3 0.5 pair_level.4.own_ref
  47.8 0.0 slice-start.3
  47.8 0.1 collective-permute-start.2
  47.9 5.0 %collective-permute-done.2.other_ref = bf16[32,16,128]{2,1,0:T(8,128)(2,1)S(1)} collective-permute-done((bf16[32,16,128]{2,1,0:T(8,128)(2,1)S(1)}, bf16[32,16,128]{2,1,0:T(8,128)(2,1)S(1)}, u32[]{:S(2)}, u32[]{:S(2)}) %collective-permute-start.2) | collective-permute-done | bytes 131104 | tf_op jit(solution)/shard_map/ppermute | solution.py:383
  52.9 0.5 pair_level.5.own_ref
  53.4 0.4 collective-permute-start.3
  53.8 6.7 %collective-permute-done.3.other_ref = bf16[32,16,128]{2,1,0:T(8,128)(2,1)S(1)} collective-permute-done((bf16[32,16,128]{2,1,0:T(8,128)(2,1)S(1)}, bf16[32,16,128]{2,1,0:T(8,128)(2,1)S(1)}, u32[]{:S(2)}, u32[]{:S(2)}) %collective-permute-start.3) | collective-permute-done | bytes 131104 | tf_op jit(solution)/shard_map/ppermute | solution.py:383
  60.4 0.0 slice-done.2
  60.5 0.0 slice-done.3
  60.5 3.6 %last_level_and_field.1 = bf16[32,16,4096]{2,1,0:T(8,128)(2,1)} custom-call(bf16[32,16,128]{2,1,0:T(8,128)(2,1)S(1)} %pair_level.5.own_ref, bf16[32,16,128]{2,1,0:T(8,128)(2,1)S(1)} %collective-permute-done.3.other_ref, bf16[9,32,64,128]{3,2,1,0:T(8,128)(2,1)S(1)} %copy-done, bf16[9,32,64,128]{3,2,1,0:T(8,128)(2,1)S(1)} %copy-done.1, ...), custom_call_target="tpu_custom_call" | custom-call | tf_op jit(solution)/shard_map/last_level_and_field/pallas_call | solution.py:338
  (6 shorter events, 0.0 us)
Async XLA Ops:
  0.0 37.9 %copy-start = (bf16[9,32,64,128]{3,2,1,0:T(8,128)(2,1)S(1)}, bf16[9,32,64,128]{3,2,1,0:T(8,128)(2,1)}, u32[]{:S(2)}) copy-start(bf16[9,32,64,128]{3,2,1,0:T(8,128)(2,1)} %self_ref.9) | copy-start | bytes 14155780
  0.0 37.9 %copy-start.1 = (bf16[9,32,64,128]{3,2,1,0:T(8,128)(2,1)S(1)}, bf16[9,32,64,128]{3,2,1,0:T(8,128)(2,1)}, u32[]{:S(2)}) copy-start(bf16[9,32,64,128]{3,2,1,0:T(8,128)(2,1)} %cross_ref.9) | copy-start | bytes 14155780
  37.9 22.6 %slice-start = ((s8[16777216]{0:T(1024)(128)(4,1)}), s8[4194304]{0:T(1024)(128)(4,1)S(1)}, s32[]{:S(2)}) async-start(s8[16777216]{0:T(1024)(128)(4,1)} %bitcast.2), calls=%async_computation.2 | async-start | bytes 8388608
  39.7 20.7 %slice-start.1 = ((s8[16777216]{0:T(1024)(128)(4,1)}), s8[4194304]{0:T(1024)(128)(4,1)S(1)}, s32[]{:S(2)}) async-start(s8[16777216]{0:T(1024)(128)(4,1)} %bitcast.2), calls=%async_computation.3 | async-start | bytes 8388608
  39.8 1.4 %collective-permute-start = (bf16[32,16,128]{2,1,0:T(8,128)(2,1)S(1)}, bf16[32,16,128]{2,1,0:T(8,128)(2,1)S(1)}, u32[]{:S(2)}, u32[]{:S(2)}) collective-permute-start(bf16[32,16,128]{2,1,0:T(8,128)(2,1)S(1)} %local_levels.1.own_ref), channel_id=1, source_target_pairs={{0,2},{2,0},{4,6},{6,4},{8,10},{10,8},{12,14},{14,12},{16,18},{18,... | collective-permute-start | bytes 393224 | tf_op jit(solution)/shard_map/ppermute | solution.py:383
  41.7 18.8 %slice-start.2 = ((s8[16777216]{0:T(1024)(128)(4,1)}), s8[4194304]{0:T(1024)(128)(4,1)S(1)}, s32[]{:S(2)}) async-start(s8[16777216]{0:T(1024)(128)(4,1)} %bitcast.2), calls=%async_computation.4 | async-start | bytes 8388608
  41.7 5.6 %collective-permute-start.1 = (bf16[32,16,128]{2,1,0:T(8,128)(2,1)S(1)}, bf16[32,16,128]{2,1,0:T(8,128)(2,1)S(1)}, u32[]{:S(2)}, u32[]{:S(2)}) collective-permute-start(bf16[32,16,128]{2,1,0:T(8,128)(2,1)S(1)} %pair_level.3.own_ref), channel_id=1, source_target_pairs={{0,4},{2,6},{4,0},{6,2},{8,12},{10,14},{12,8},{14,10},{16,20},{18,... | collective-permute-start | bytes 393224 | tf_op jit(solution)/shard_map/ppermute | solution.py:383
  47.8 12.6 %slice-start.3 = ((s8[16777216]{0:T(1024)(128)(4,1)}), s8[4194304]{0:T(1024)(128)(4,1)S(1)}, s32[]{:S(2)}) async-start(s8[16777216]{0:T(1024)(128)(4,1)} %bitcast.2), calls=%async_computation.5 | async-start | bytes 8388608
  47.8 5.0 %collective-permute-start.2 = (bf16[32,16,128]{2,1,0:T(8,128)(2,1)S(1)}, bf16[32,16,128]{2,1,0:T(8,128)(2,1)S(1)}, u32[]{:S(2)}, u32[]{:S(2)}) collective-permute-start(bf16[32,16,128]{2,1,0:T(8,128)(2,1)S(1)} %pair_level.4.own_ref), channel_id=1, source_target_pairs={{0,8},{2,10},{4,12},{6,14},{8,0},{10,2},{12,4},{14,6},{16,24},{18,... | collective-permute-start | bytes 393224 | tf_op jit(solution)/shard_map/ppermute | solution.py:383
  53.4 7.1 %collective-permute-start.3 = (bf16[32,16,128]{2,1,0:T(8,128)(2,1)S(1)}, bf16[32,16,128]{2,1,0:T(8,128)(2,1)S(1)}, u32[]{:S(2)}, u32[]{:S(2)}) collective-permute-start(bf16[32,16,128]{2,1,0:T(8,128)(2,1)S(1)} %pair_level.5.own_ref), channel_id=1, source_target_pairs={{0,16},{2,18},{4,20},{6,22},{8,24},{10,26},{12,28},{14,30},{16,0},... | collective-permute-start | bytes 393224 | tf_op jit(solution)/shard_map/ppermute | solution.py:383

commit v3 on v2

--- a/solution.py
+++ b/solution.py
@@ -14,6 +14,7 @@
 UNROLL = 8
 ROWS = 16
 LEAF_VMEM = 48
+LAST_PARTS = 1
 
 
 def dot(a, b):
@@ -175,7 +176,7 @@
             pltpu.VMEM((1, boxes), jnp.int32),
             pltpu.VMEM(bank.shape, BF16),
             pltpu.VMEM(leaf_factor.shape, BF16),
-            pltpu.VMEM((box_dev * stored, rank2), F32),
+            pltpu.VMEM(((box_dev + 1) * stored, rank2), F32),
             pltpu.SMEM((stored // ROWS,), jnp.int32),
             pltpu.SMEM((stored // ROWS,), jnp.int32),
             pltpu.SMEM((stored // ROWS,), jnp.int32),
@@ -217,7 +218,7 @@
 def local_kernel(local_bits, leaves_ref, self_ref, cross_ref, out_ref, wide, state):
     cols, slots, rank2 = leaves_ref.shape
     rank = rank2 // 2
-    wide[...] = leaves_ref[...].astype(F32).reshape(cols * slots, rank2)
+    wide[: cols * slots, :] = leaves_ref[...].astype(F32).reshape(cols * slots, rank2)
     for s in range(slots):
         state[0, s] = wide[pl.ds(s, cols, stride=slots), :]
     for level in range(local_bits):
@@ -249,7 +250,7 @@
         in_specs=[pl.BlockSpec(memory_space=pltpu.VMEM)] * 3,
         out_specs=pl.BlockSpec(memory_space=pltpu.VMEM),
         scratch_shapes=[
-            pltpu.VMEM((cols * slots, rank2), F32),
+            pltpu.VMEM(((cols + 1) * slots, rank2), F32),
             pltpu.VMEM((2, slots, cols, rank2), F32),
         ],
         compiler_params=pltpu.CompilerParams(vmem_limit_bytes=16 * MIB),
@@ -257,28 +258,70 @@
     )(leaves, self_factor, cross_factor)
 
 
-def mix_slot(level, s, own_ref, other_ref, self_ref, cross_ref):
+def turn_kernel(level, _, self_ref, cross_ref, out_ref):
+    slots, rank, rank2 = out_ref.shape[1:]
+    low = lanes_below((rank, rank2), rank)
+
+    def step(s, _):
+        for k, factor in enumerate((self_ref, cross_ref)):
+            turned = pltpu.roll(factor[level, s].astype(F32), rank, 1)
+            out_ref[k, s] = jnp.where(low, -turned, turned).astype(BF16)
+        return 0
+
+    lax.fori_loop(0, slots, step, 0, unroll=8)
+
+
+def turn_step(level, after, self_factor, cross_factor):
+    shape = (2,) + self_factor.shape[1:]
+    size = 2 * 2 * shape[1] * shape[2] * shape[3]
+    return pl.pallas_call(
+        functools.partial(turn_kernel, level),
+        out_shape=jax.ShapeDtypeStruct(shape, BF16),
+        in_specs=[
+            pl.BlockSpec(memory_space=pl.ANY),
+            pl.BlockSpec(memory_space=pltpu.VMEM),
+            pl.BlockSpec(memory_space=pltpu.VMEM),
+        ],
+        out_specs=pl.BlockSpec(memory_space=pltpu.VMEM),
+        cost_estimate=pl.CostEstimate(flops=size, bytes_accessed=2 * size, transcendentals=0),
+        compiler_params=pltpu.CompilerParams(vmem_limit_bytes=12 * MIB),
+        name="turn_factors",
+    )(after, self_factor, cross_factor)
+
+
+def mix_pair(level, offset, i, own_ref, other_ref, self_ref, cross_ref, turned_ref):
     cols, rank2 = own_ref.shape[1:]
-    rank = rank2 // 2
-    rows = stack_pair(own_ref[s].astype(F32), other_ref[s].astype(F32), rank)
-    product = dot(rows, jnp.concatenate([self_ref[level, s], cross_ref[level, s]], axis=0))
-    return combine(product[:cols], product[cols:], rank)
-
-
-def pair_kernel(level, own_ref, other_ref, self_ref, cross_ref, out_ref):
-    for s in range(own_ref.shape[0]):
-        out_ref[s] = mix_slot(level, s, own_ref, other_ref, self_ref, cross_ref).astype(BF16)
-
-
-def pair_step(level, own, other, self_factor, cross_factor):
+    rows, factors = [], []
+    for k in (i, i + 1):
+        s = offset + k
+        rows.append(jnp.concatenate([own_ref[k], other_ref[k]], axis=1))
+        factors.append(
+            jnp.concatenate(
+                [self_ref[level, s], turned_ref[0, s], cross_ref[level, s], turned_ref[1, s]], axis=0
+            )
+        )
+    both = dot(jnp.concatenate(rows, axis=0), jnp.concatenate(factors, axis=1))
+    return both[:cols, :rank2], both[cols:, rank2:]
+
+
+def pair_kernel(level, own_ref, other_ref, self_ref, cross_ref, turned_ref, *out_refs):
+    size = out_refs[0].shape[0]
+    for i in range(0, own_ref.shape[0], 2):
+        pair = mix_pair(level, 0, i, own_ref, other_ref, self_ref, cross_ref, turned_ref)
+        for k in range(2):
+            out_refs[(i + k) // size][(i + k) % size] = pair[k].astype(BF16)
+
+
+def pair_step(level, parts, own, other, self_factor, cross_factor, turned):
+    shape = (own.shape[0] // parts,) + own.shape[1:]
     return pl.pallas_call(
         functools.partial(pair_kernel, level),
-        out_shape=jax.ShapeDtypeStruct(own.shape, BF16),
-        in_specs=[pl.BlockSpec(memory_space=pltpu.VMEM)] * 4,
-        out_specs=pl.BlockSpec(memory_space=pltpu.VMEM),
+        out_shape=(jax.ShapeDtypeStruct(shape, BF16),) * parts,
+        in_specs=[pl.BlockSpec(memory_space=pltpu.VMEM)] * 5,
+        out_specs=(pl.BlockSpec(memory_space=pltpu.VMEM),) * parts,
         compiler_params=pltpu.CompilerParams(vmem_limit_bytes=16 * MIB),
         name="pair_level",
-    )(own, other, self_factor, cross_factor)
+    )(own, other, self_factor, cross_factor, turned)
 
 
 GROUP = 4
@@ -286,17 +329,29 @@
 
 
 def field_kernel(
-    level, own_ref, other_ref, self_ref, cross_ref, target_ref, out_ref, final, result, sems
+    level,
+    offset,
+    own_ref,
+    other_ref,
+    self_ref,
+    cross_ref,
+    turned_ref,
+    target_ref,
+    *rest,
 ):
+    out_ref, final, result, sems = rest[-4:]
     slots, cols, rank2 = own_ref.shape
     rank = rank2 // 2
     points = target_ref.shape[-1] // 2
-    for s in range(slots):
-        final[s] = mix_slot(level, s, own_ref, other_ref, self_ref, cross_ref)
+    for i in range(0, slots, 2):
+        pair = mix_pair(level, offset, i, own_ref, other_ref, self_ref, cross_ref, turned_ref)
+        final[i] = pair[0]
+        final[i + 1] = pair[1]
 
     def out_copy(q):
         part = pl.ds(q * GROUP, GROUP)
-        return pltpu.make_async_copy(result.at[part], out_ref.at[part], sems.at[q])
+        there = pl.ds(offset + q * GROUP, GROUP)
+        return pltpu.make_async_copy(result.at[part], out_ref.at[there], sems.at[q])
 
     def group(q):
         rows = []
@@ -312,7 +367,7 @@
                 jnp.concatenate([block if j == i // 2 else empty for j in range(GROUP // 2)], axis=1)
             )
         rows = jnp.concatenate(rows, axis=0).astype(BF16)
-        part = pl.ds(q * GROUP, GROUP)
+        part = pl.ds(offset + q * GROUP, GROUP)
         for start in range(0, points, TILE):
             real_part = target_ref[part, :, pl.ds(start, TILE)].reshape(GROUP * rank, TILE)
             imag_part = target_ref[part, :, pl.ds(points + start, TILE)].reshape(GROUP * rank, TILE)
@@ -332,28 +387,31 @@
         out_copy(q).wait()
 
 
-def field_step(level, own, other, self_factor, cross_factor, target_factor):
+def field_step(level, offset, own, other, self_factor, cross_factor, turned, target, filled):
     slots, cols, rank2 = own.shape
-    width = target_factor.shape[-1]
-    return pl.pallas_call(
-        functools.partial(field_kernel, level),
-        out_shape=jax.ShapeDtypeStruct((slots, cols, width), BF16),
-        in_specs=[pl.BlockSpec(memory_space=pltpu.VMEM)] * 5,
+    width = target.shape[-1]
+    in_specs = [pl.BlockSpec(memory_space=pltpu.VMEM)] * 6
+    operands = [own, other, self_factor, cross_factor, turned]
+    operands.append(pltpu.with_memory_space_constraint(target, pltpu.VMEM))
+    aliases = {}
+    if filled is not None:
+        in_specs.append(pl.BlockSpec(memory_space=pl.ANY))
+        operands.append(filled)
+        aliases = {6: 0}
+    return pl.pallas_call(
+        functools.partial(field_kernel, level, offset),
+        out_shape=jax.ShapeDtypeStruct((target.shape[0], cols, width), BF16),
+        in_specs=in_specs,
         out_specs=pl.BlockSpec(memory_space=pl.ANY),
         scratch_shapes=[
             pltpu.VMEM((slots, cols, rank2), F32),
             pltpu.VMEM((slots, cols, width), BF16),
             pltpu.SemaphoreType.DMA((slots // GROUP,)),
         ],
-        compiler_params=pltpu.CompilerParams(vmem_limit_bytes=22 * MIB),
+        input_output_aliases=aliases,
+        compiler_params=pltpu.CompilerParams(vmem_limit_bytes=20 * MIB),
         name="last_level_and_field",
-    )(
-        own,
-        other,
-        self_factor,
-        cross_factor,
-        pltpu.with_memory_space_constraint(target_factor, pltpu.VMEM),
-    )
+    )(*operands)
 
 
 def per_device(bank, pick, slot_box, leaf_factor, self_factor, cross_factor, target_factor):
@@ -377,13 +435,24 @@
     if parts > 1:
         leaves = leaves.reshape(cols, parts, box_dev, width).transpose(0, 2, 1, 3)
         leaves = leaves.reshape(cols, box_dev, rank2)
-    current = local_step(local_bits, leaves, self_factor, cross_factor)
+    current = (local_step(local_bits, leaves, self_factor, cross_factor),)
     for level in range(local_bits, levels):
         bit = 1 << (level - local_bits)
-        other = lax.ppermute(current, "box", [(i, i ^ bit) for i in range(devices)])
+        route = [(i, i ^ bit) for i in range(devices)]
+        turned = turn_step(level, current[0], self_factor, cross_factor)
+        others = [lax.ppermute(part, "box", route) for part in current]
         if level < levels - 1:
-            current = pair_step(level, current, other, self_factor, cross_factor)
-    return field_step(level, current, other, self_factor, cross_factor, target_factor)
+            parts = LAST_PARTS if level == levels - 2 else 1
+            current = pair_step(
+                level, parts, *current, *others, self_factor, cross_factor, turned
+            )
+    field, offset = None, 0
+    for own, other in zip(current, others, strict=True):
+        field = field_step(
+            level, offset, own, other, self_factor, cross_factor, turned, target_factor, field
+        )
+        offset += own.shape[0]
+    return field
 
 
 def solution(mesh):

time: 64.1 us -> 63.8 us (level)
  waiting for transfers between devices: 18.5 us -> 16.2 us
  Pallas kernels: 16 us -> 17 us
  blocking collectives: 28.8 us -> 29.5 us
    ppermute x4, waiting for transfers between devices: 18.5 us -> 16.2 us  [per_device(): others = [lax.ppermute(part, 'box', route) for part in current]]
    pallas_call x4 -> x8, Pallas kernels: 5.09 us -> 7.08 us  [the longest x1 3.58 us: field_step(): pl.pallas_call(functools.partial(field_kernel, level, offset), out_shape=...]
    pallas_call x1, Pallas kernels: 8.73 us -> 7.77 us  [leaf_step(): pl.pallas_call(functools.partial(leaf_kernel, cols), out_shape=(jax.Shape...]
    all_to_all x1, blocking collectives: 18.3 us -> 18.9 us  [per_device(): sent = lax.all_to_all(sent, ('box', 'tx'), 0, 0, tiled=True)]
  transfers between devices with their start and end apart: 4 -> 4, of which waited for: 4 -> 4; matrix products, arithmetic and copies ran while one was open for 0% -> 0% of each run, Pallas kernels for 0% -> 4%
where the time goes in v3:
time: 63.8 us; the launch traced here: 63.5 us
  blocking collectives  29.5 us (46%)
  Pallas kernels  17 us (27%)
  waiting for transfers between devices  16.2 us (25%)
    all_to_all x1, blocking collectives, per_device(): sent = lax.all_to_all(sent, ('box', 'tx'), 0, 0, tiled=True)  18.9 us
    ppermute x4, waiting for transfers between devices, per_device(): others = [lax.ppermute(part, 'box', route) for part in current]  16.2 us
    all_to_all x1, blocking collectives, per_device(): leaves = lax.all_to_all(ordered, 'box', 0, 0, tiled=True)  10.5 us
    pallas_call x1, Pallas kernels, leaf_step(): pl.pallas_call(functools.partial(leaf_kernel, cols), out_shape=(jax.Shape...  7.77 us
    pallas_call x1, Pallas kernels, field_step(): pl.pallas_call(functools.partial(field_kernel, level, offset), out_shape=...  3.58 us
    pallas_call x4, Pallas kernels, turn_step(): pl.pallas_call(functools.partial(turn_kernel, level), out_shape=jax.Shape...  2.25 us
    pallas_call x1, Pallas kernels, local_step(): pl.pallas_call(functools.partial(local_kernel, local_bits), out_shape=jax...  1.87 us
  transfers between devices with their start and end apart: 4, of which 4 were waited for; matrix products, arithmetic and copies ran while one was open for 0% of the time, Pallas kernels for 4%

profile of v3, /device:TPU:0, one launch (start us, length us, event | category | flops | bytes accessed | tf_op | source)
XLA Modules:
  0.0 63.5 jit_solution(11099925347660952155)
XLA Ops:
  0.0 7.8 %select_and_leaf.1 = (bf16[32,32,128]{2,1,0:T(8,128)(2,1)S(1)}, bf16[512,512]{1,0:T(8,128)(2,1)S(1)}) custom-call(s32[32]{0:T(128)} %pick_hbm.1, s32[1,512]{1,0:T(1,128)} %bitcast.5, bf16[32,256,1024]{2,1,0:T(8,128)(2,1)} %bank_ref.1, bf16[32,512,128]{2,1,0:T(8,128)(2,1)} %leaf_ref.1), custom_call_target="tpu_custom_call" | custom-call | tf_op jit(solution)/shard_map/select_and_leaf/pallas_call | solution.py:158
  7.8 18.9 %all_to_all.10 = bf16[32,32,128]{2,1,0:T(8,128)(2,1)S(1)} all-to-all(bf16[32,32,128]{2,1,0:T(8,128)(2,1)S(1)} %get-tuple-element.8), channel_id=1, replica_groups=mesh['box'=16,'tx'=2] {'box','tx'}, dimensions={0} | all-to-all | bytes 524288 | tf_op jit(solution)/shard_map/all_to_all | solution.py:432
  26.7 0.3 leaf_order.1
  27.0 10.5 %all_to_all.11.leaves_ref = bf16[16,32,128]{2,1,0:T(8,128)(2,1)S(1)} all-to-all(bf16[16,32,128]{2,1,0:T(8,128)(2,1)S(1)} %leaf_order.1), channel_id=1, replica_groups=mesh['box'=16,'tx'=2] {'box'}, dimensions={0} | all-to-all | bytes 262144 | tf_op jit(solution)/shard_map/all_to_all | solution.py:434
  37.6 1.9 %local_levels.1._.own_ref = bf16[32,16,128]{2,1,0:T(8,128)(2,1)S(1)} custom-call(bf16[16,32,128]{2,1,0:T(8,128)(2,1)S(1)} %all_to_all.11.leaves_ref, bf16[9,32,64,128]{3,2,1,0:T(8,128)(2,1)S(1)} %copy-done, bf16[9,32,64,128]{3,2,1,0:T(8,128)(2,1)S(1)} %copy-done.1), custom_call_target="tpu_custom_call" | custom-call | tf_op jit(solution)/shard_map/local_levels/pallas_call | solution.py:247
  39.4 0.1 collective-permute-start
  39.5 0.6 turn_factors.4.turned_ref
  40.1 0.8 %collective-permute-done.other_ref = bf16[32,16,128]{2,1,0:T(8,128)(2,1)S(1)} collective-permute-done((bf16[32,16,128]{2,1,0:T(8,128)(2,1)S(1)}, bf16[32,16,128]{2,1,0:T(8,128)(2,1)S(1)}, u32[]{:S(2)}, u32[]{:S(2)}) %collective-permute-start) | collective-permute-done | bytes 131104 | tf_op jit(solution)/shard_map/ppermute | solution.py:443
  40.9 0.4 pair_level.3._.own_ref
  41.3 0.1 collective-permute-start.1
  41.4 0.6 turn_factors.5.turned_ref
  41.9 5.0 %collective-permute-done.1.other_ref = bf16[32,16,128]{2,1,0:T(8,128)(2,1)S(1)} collective-permute-done((bf16[32,16,128]{2,1,0:T(8,128)(2,1)S(1)}, bf16[32,16,128]{2,1,0:T(8,128)(2,1)S(1)}, u32[]{:S(2)}, u32[]{:S(2)}) %collective-permute-start.1) | collective-permute-done | bytes 131104 | tf_op jit(solution)/shard_map/ppermute | solution.py:443
  46.9 0.4 pair_level.4._.own_ref
  47.3 0.1 collective-permute-start.2
  47.4 0.0 slice-start
  47.4 0.6 turn_factors.6.turned_ref
  48.0 0.0 slice-start.2
  48.0 4.3 %collective-permute-done.2.other_ref = bf16[32,16,128]{2,1,0:T(8,128)(2,1)S(1)} collective-permute-done((bf16[32,16,128]{2,1,0:T(8,128)(2,1)S(1)}, bf16[32,16,128]{2,1,0:T(8,128)(2,1)S(1)}, u32[]{:S(2)}, u32[]{:S(2)}) %collective-permute-start.2) | collective-permute-done | bytes 131104 | tf_op jit(solution)/shard_map/ppermute | solution.py:443
  52.4 0.4 pair_level.5._.own_ref
  52.8 0.0 slice-start.3
  52.8 0.4 collective-permute-start.3
  53.2 0.6 turn_factors.7.turned_ref
  53.8 6.1 %collective-permute-done.3.other_ref = bf16[32,16,128]{2,1,0:T(8,128)(2,1)S(1)} collective-permute-done((bf16[32,16,128]{2,1,0:T(8,128)(2,1)S(1)}, bf16[32,16,128]{2,1,0:T(8,128)(2,1)S(1)}, u32[]{:S(2)}, u32[]{:S(2)}) %collective-permute-start.3) | collective-permute-done | bytes 131104 | tf_op jit(solution)/shard_map/ppermute | solution.py:443
  59.9 3.6 %last_level_and_field.1 = bf16[32,16,4096]{2,1,0:T(8,128)(2,1)} custom-call(bf16[32,16,128]{2,1,0:T(8,128)(2,1)S(1)} %pair_level.5._.own_ref, bf16[32,16,128]{2,1,0:T(8,128)(2,1)S(1)} %collective-permute-done.3.other_ref, bf16[9,32,64,128]{3,2,1,0:T(8,128)(2,1)S(1)} %copy-done, bf16[9,32,64,128]{3,2,1,0:T(8,128)(2,1)S(1)} %copy-done.1, ...), custom_call_target="tpu_custom_call" | custom-call | tf_op jit(solution)/shard_map/last_level_and_field/pallas_call | solution.py:401
  (10 shorter events, 0.0 us)
Async XLA Ops:
  0.0 37.6 %copy-start = (bf16[9,32,64,128]{3,2,1,0:T(8,128)(2,1)S(1)}, bf16[9,32,64,128]{3,2,1,0:T(8,128)(2,1)}, u32[]{:S(2)}) copy-start(bf16[9,32,64,128]{3,2,1,0:T(8,128)(2,1)} %self_ref.17) | copy-start | bytes 14155780
  0.0 37.6 %copy-start.1 = (bf16[9,32,64,128]{3,2,1,0:T(8,128)(2,1)S(1)}, bf16[9,32,64,128]{3,2,1,0:T(8,128)(2,1)}, u32[]{:S(2)}) copy-start(bf16[9,32,64,128]{3,2,1,0:T(8,128)(2,1)} %cross_ref.17) | copy-start | bytes 14155780
  39.4 1.4 %collective-permute-start = (bf16[32,16,128]{2,1,0:T(8,128)(2,1)S(1)}, bf16[32,16,128]{2,1,0:T(8,128)(2,1)S(1)}, u32[]{:S(2)}, u32[]{:S(2)}) collective-permute-start(bf16[32,16,128]{2,1,0:T(8,128)(2,1)S(1)} %local_levels.1._.own_ref), channel_id=1, source_target_pairs={{0,2},{2,0},{4,6},{6,4},{8,10},{10,8},{12,14},{14,12},{16,18},{18,... | collective-permute-start | bytes 393224 | tf_op jit(solution)/shard_map/ppermute | solution.py:443
  41.3 5.6 %collective-permute-start.1 = (bf16[32,16,128]{2,1,0:T(8,128)(2,1)S(1)}, bf16[32,16,128]{2,1,0:T(8,128)(2,1)S(1)}, u32[]{:S(2)}, u32[]{:S(2)}) collective-permute-start(bf16[32,16,128]{2,1,0:T(8,128)(2,1)S(1)} %pair_level.3._.own_ref), channel_id=1, source_target_pairs={{0,4},{2,6},{4,0},{6,2},{8,12},{10,14},{12,8},{14,10},{16,20},{18,... | collective-permute-start | bytes 393224 | tf_op jit(solution)/shard_map/ppermute | solution.py:443
  47.3 5.0 %collective-permute-start.2 = (bf16[32,16,128]{2,1,0:T(8,128)(2,1)S(1)}, bf16[32,16,128]{2,1,0:T(8,128)(2,1)S(1)}, u32[]{:S(2)}, u32[]{:S(2)}) collective-permute-start(bf16[32,16,128]{2,1,0:T(8,128)(2,1)S(1)} %pair_level.4._.own_ref), channel_id=1, source_target_pairs={{0,8},{2,10},{4,12},{6,14},{8,0},{10,2},{12,4},{14,6},{16,24},{18,... | collective-permute-start | bytes 393224 | tf_op jit(solution)/shard_map/ppermute | solution.py:443
  47.4 12.5 %slice-start = ((s8[16777216]{0:T(1024)(128)(4,1)}), s8[4194304]{0:T(1024)(128)(4,1)S(1)}, s32[]{:S(2)}) async-start(s8[16777216]{0:T(1024)(128)(4,1)} %bitcast.2), calls=%async_computation.2 | async-start | bytes 8388608
  47.4 12.5 %slice-start.1 = ((s8[16777216]{0:T(1024)(128)(4,1)}), s8[4194304]{0:T(1024)(128)(4,1)S(1)}, s32[]{:S(2)}) async-start(s8[16777216]{0:T(1024)(128)(4,1)} %bitcast.2), calls=%async_computation.3 | async-start | bytes 8388608
  48.0 11.9 %slice-start.2 = ((s8[16777216]{0:T(1024)(128)(4,1)}), s8[4194304]{0:T(1024)(128)(4,1)S(1)}, s32[]{:S(2)}) async-start(s8[16777216]{0:T(1024)(128)(4,1)} %bitcast.2), calls=%async_computation.4 | async-start | bytes 8388608
  52.8 7.1 %slice-start.3 = ((s8[16777216]{0:T(1024)(128)(4,1)}), s8[4194304]{0:T(1024)(128)(4,1)S(1)}, s32[]{:S(2)}) async-start(s8[16777216]{0:T(1024)(128)(4,1)} %bitcast.2), calls=%async_computation.5 | async-start | bytes 8388608
  52.8 7.1 %collective-permute-start.3 = (bf16[32,16,128]{2,1,0:T(8,128)(2,1)S(1)}, bf16[32,16,128]{2,1,0:T(8,128)(2,1)S(1)}, u32[]{:S(2)}, u32[]{:S(2)}) collective-permute-start(bf16[32,16,128]{2,1,0:T(8,128)(2,1)S(1)} %pair_level.5._.own_ref), channel_id=1, source_target_pairs={{0,16},{2,18},{4,20},{6,22},{8,24},{10,26},{12,28},{14,30},{16,0},... | collective-permute-start | bytes 393224 | tf_op jit(solution)/shard_map/ppermute | solution.py:443

commit v4 on v3

--- a/solution.py
+++ b/solution.py
@@ -11,7 +11,6 @@
 F32 = jnp.float32
 MIB = 1 << 20
 BATCH = 8
-UNROLL = 8
 ROWS = 16
 LEAF_VMEM = 48
 LAST_PARTS = 1
@@ -49,6 +48,8 @@
     slot_ref,
     bank,
     leaf,
+    chooser,
+    chosen,
     coefs,
     present,
     wanted,
@@ -57,13 +58,14 @@
     bank_sems,
     leaf_sems,
 ):
-    box_dev, stored, unknowns = bank_ref.shape
-    unknowns //= 2
+    box_dev, stored, width = bank_ref.shape
+    unknowns = width // 2
     rank = leaf_ref.shape[-1] // 2
     picked = pick_ref.shape[0]
     base = lax.axis_index("tx") * stored
+    row_groups = stored // ROWS
+    few = row_groups * 3 // 4
     batches = box_dev // BATCH
-    row_groups = stored // ROWS
 
     def leaf_copy(g):
         part = pl.ds(g * BATCH, BATCH)
@@ -81,7 +83,8 @@
     slot_copy = pltpu.make_async_copy(slot_hbm, slot_ref, index_sems.at[1])
     pick_copy.start()
     slot_copy.start()
-    leaf_copy(0).start()
+    for g in range(2):
+        leaf_copy(g).start()
     pick_copy.wait()
     for k in range(row_groups):
         present[k] = 0
@@ -98,16 +101,29 @@
         rank_of[k] = count
         count = count + present[k]
 
-    def start(g, _):
-        lax.fori_loop(0, count, lambda j, _: (bank_copy(g, j).start(), 0)[1], 0)
-
-        @pl.when(g > 0)
-        def _():
+    for g in range(batches):
+        lax.fori_loop(0, count, lambda j, _, g=g: (bank_copy(g, j).start(), 0)[1], 0)
+        if g > 1:
             leaf_copy(g).start()
 
+    row = lax.broadcasted_iota(jnp.int32, (picked, stored), 0)
+    column = lax.broadcasted_iota(jnp.int32, (picked, stored), 1)
+    target = jnp.full((picked, stored), -1, jnp.int32)
+    for c in range(picked):
+        place = pick_ref[c] - base
+        held = jnp.logical_and(place >= 0, place < stored)
+        place = jnp.where(held, place, 0)
+        place = jnp.where(held, rank_of[place // ROWS] * ROWS + place % ROWS, -1)
+        target = jnp.where(row == c, place, target)
+    chooser[...] = (target == column).astype(F32).astype(BF16)
+
+    def blank(j, _):
+        rows = pl.ds(pl.multiple_of(j * ROWS, ROWS), ROWS)
+        for b in range(box_dev):
+            bank[b, rows, :] = jnp.zeros((ROWS, width), BF16)
         return 0
 
-    lax.fori_loop(0, batches, start, 0)
+    lax.fori_loop(count, jnp.where(count <= few, few, row_groups), blank, 0)
 
     slot_copy.wait()
     boxes = slot_ref.shape[1]
@@ -116,44 +132,44 @@
         hit = (box == slot_ref[:, c : c + 128]).astype(F32)
         perm_ref[c : c + 128, :] = hit.T.astype(BF16)
 
-    def map_batch(g, _):
-        leaf_copy(g).wait()
-        lax.fori_loop(0, count, lambda j, _: (bank_copy(g, j).wait(), 0)[1], 0)
-
-        def map_boxes(rows):
-            def step(k, _):
-                for i in range(UNROLL):
-                    b = g * BATCH + k * UNROLL + i
-                    first = dot(bank[b, :rows, :unknowns], leaf[b])
-                    second = dot(bank[b, :rows, unknowns:], leaf[b])
-                    place = pl.ds(pl.multiple_of(b * stored, stored), rows)
-                    coefs[place, :] = combine(first, second, rank)
-                return 0
-
-            lax.fori_loop(0, BATCH // UNROLL, step, 0)
-
-        quarter = row_groups // 4
-        for part in range(2, 5):
-            low = 0 if part == 2 else (part - 1) * quarter
-            fits = jnp.logical_and(count > low, count <= part * quarter)
-            pl.when(fits)(functools.partial(map_boxes, part * quarter * ROWS))
-        return 0
-
-    lax.fori_loop(0, batches, map_batch, 0)
+    def select(g, rows):
+        for b in range(g * BATCH, (g + 1) * BATCH):
+            values = dot(chooser[:, :rows], bank[b, :rows, :]).astype(BF16)
+            chosen[b % (2 * BATCH)] = jnp.concatenate(
+                [values[:, :unknowns], values[:, unknowns:]], axis=0
+            )
+
+    def map_boxes(g):
+        for b in range(g * BATCH, (g + 1) * BATCH):
+            product = dot(chosen[b % (2 * BATCH)], leaf[b])
+            coefs[b * picked : (b + 1) * picked, :] = combine(
+                product[:picked], product[picked:], rank
+            )
+
+    def advance(g, rows):
+        select(g, rows)
+        if g > 0:
+            map_boxes(g - 1)
+
+    for g in range(batches):
+        if g > 0:
+            leaf_copy(g - 1).wait()
+        lax.fori_loop(0, count, lambda j, _, g=g: (bank_copy(g, j).wait(), 0)[1], 0)
+        pl.when(count <= few)(functools.partial(advance, g, few * ROWS))
+        pl.when(count > few)(functools.partial(advance, g, stored))
+    leaf_copy(batches - 1).wait()
+    map_boxes(batches - 1)
     groups = picked // cols
     for c in range(picked):
-        place = pick_ref[c] - base
-        held = jnp.logical_and(place >= 0, place < stored)
-        place = jnp.where(held, place, 0)
-        row = jnp.where(held, rank_of[place // ROWS] * ROWS + place % ROWS, 0)
-        rows = coefs[pl.ds(row, box_dev, stride=stored), :]
-        out_ref[(c % cols) * groups + c // cols] = jnp.where(held, rows, 0.0).astype(BF16)
+        rows = coefs[pl.ds(c, box_dev, stride=picked), :]
+        out_ref[(c % cols) * groups + c // cols] = rows.astype(BF16)
 
 
 def leaf_step(cols, bank, pick, slot_box, leaf_factor):
-    box_dev, stored, _ = bank.shape
+    box_dev, stored, width = bank.shape
     picked = pick.shape[0]
     boxes = slot_box.shape[0]
+    steps = box_dev // BATCH
     rank2 = leaf_factor.shape[-1]
     return pl.pallas_call(
         functools.partial(leaf_kernel, cols),
@@ -161,12 +177,7 @@
             jax.ShapeDtypeStruct((picked, box_dev, rank2), BF16),
             jax.ShapeDtypeStruct((boxes, boxes), BF16),
         ),
-        in_specs=[
-            pl.BlockSpec(memory_space=pltpu.HBM),
-            pl.BlockSpec(memory_space=pltpu.HBM),
-            pl.BlockSpec(memory_space=pltpu.HBM),
-            pl.BlockSpec(memory_space=pltpu.HBM),
-        ],
+        in_specs=[pl.BlockSpec(memory_space=pltpu.HBM)] * 4,
         out_specs=(
             pl.BlockSpec(memory_space=pltpu.VMEM),
             pl.BlockSpec(memory_space=pltpu.VMEM),
@@ -176,21 +187,23 @@
             pltpu.VMEM((1, boxes), jnp.int32),
             pltpu.VMEM(bank.shape, BF16),
             pltpu.VMEM(leaf_factor.shape, BF16),
-            pltpu.VMEM(((box_dev + 1) * stored, rank2), F32),
+            pltpu.VMEM((picked, stored), BF16),
+            pltpu.VMEM((2 * BATCH, 2 * picked, width // 2), BF16),
+            pltpu.VMEM(((box_dev + 1) * picked, rank2), F32),
             pltpu.SMEM((stored // ROWS,), jnp.int32),
             pltpu.SMEM((stored // ROWS,), jnp.int32),
             pltpu.SMEM((stored // ROWS,), jnp.int32),
             pltpu.SemaphoreType.DMA((2,)),
-            pltpu.SemaphoreType.DMA((box_dev // BATCH, stored // ROWS)),
-            pltpu.SemaphoreType.DMA((box_dev // BATCH,)),
+            pltpu.SemaphoreType.DMA((steps, stored // ROWS)),
+            pltpu.SemaphoreType.DMA((steps,)),
         ],
         compiler_params=pltpu.CompilerParams(vmem_limit_bytes=LEAF_VMEM * MIB),
         name="select_and_leaf",
     )(
-        pltpu.with_memory_space_constraint(pick, pltpu.HBM),
-        pltpu.with_memory_space_constraint(slot_box.reshape(1, boxes), pltpu.HBM),
-        pltpu.with_memory_space_constraint(bank, pltpu.HBM),
-        pltpu.with_memory_space_constraint(leaf_factor, pltpu.HBM),
+        *(
+            pltpu.with_memory_space_constraint(array, pltpu.HBM)
+            for array in (pick, slot_box.reshape(1, boxes), bank, leaf_factor)
+        )
     )
 
 

time: 63.8 us -> 63.4 us (level)
  blocking collectives: 29.5 us -> 28.2 us
  Pallas kernels: 17 us -> 17.7 us
    all_to_all x1, blocking collectives: 18.9 us -> 17.6 us  [per_device(): sent = lax.all_to_all(sent, ('box', 'tx'), 0, 0, tiled=True)]
    pallas_call x1, Pallas kernels: 7.77 us -> 8.49 us  [leaf_step(): pl.pallas_call(functools.partial(leaf_kernel, cols), out_shape=(jax.Shape...]
where the time goes in v4:
time: 63.4 us; the launch traced here: 63 us
  blocking collectives  28.2 us (44%)
  Pallas kernels  17.7 us (28%)
  waiting for transfers between devices  16.2 us (26%)
    all_to_all x1, blocking collectives, per_device(): sent = lax.all_to_all(sent, ('box', 'tx'), 0, 0, tiled=True)  17.6 us
    ppermute x4, waiting for transfers between devices, per_device(): others = [lax.ppermute(part, 'box', route) for part in current]  16.2 us
    all_to_all x1, blocking collectives, per_device(): leaves = lax.all_to_all(ordered, 'box', 0, 0, tiled=True)  10.5 us
    pallas_call x1, Pallas kernels, leaf_step(): pl.pallas_call(functools.partial(leaf_kernel, cols), out_shape=(jax.Shape...  8.49 us
    pallas_call x1, Pallas kernels, field_step(): pl.pallas_call(functools.partial(field_kernel, level, offset), out_shape=...  3.58 us
    pallas_call x4, Pallas kernels, turn_step(): pl.pallas_call(functools.partial(turn_kernel, level), out_shape=jax.Shape...  2.25 us
    pallas_call x1, Pallas kernels, local_step(): pl.pallas_call(functools.partial(local_kernel, local_bits), out_shape=jax...  1.87 us
  transfers between devices with their start and end apart: 4, of which 4 were waited for; matrix products, arithmetic and copies ran while one was open for 0% of the time, Pallas kernels for 4%

profile of v4, /device:TPU:0, one launch (start us, length us, event | category | flops | bytes accessed | tf_op | source)
XLA Modules:
  0.0 63.0 jit_solution(16281893875927002454)
XLA Ops:
  0.0 8.5 %select_and_leaf.1 = (bf16[32,32,128]{2,1,0:T(8,128)(2,1)S(1)}, bf16[512,512]{1,0:T(8,128)(2,1)S(1)}) custom-call(s32[32]{0:T(128)} %pick_hbm.1, s32[1,512]{1,0:T(1,128)} %bitcast.5, bf16[32,256,1024]{2,1,0:T(8,128)(2,1)} %bank_ref.1, bf16[32,512,128]{2,1,0:T(8,128)(2,1)} %leaf_ref.1), custom_call_target="tpu_custom_call" | custom-call | tf_op jit(solution)/shard_map/select_and_leaf/pallas_call | solution.py:174
  8.5 17.6 %all_to_all.10 = bf16[32,32,128]{2,1,0:T(8,128)(2,1)S(1)} all-to-all(bf16[32,32,128]{2,1,0:T(8,128)(2,1)S(1)} %get-tuple-element.8), channel_id=1, replica_groups=mesh['box'=16,'tx'=2] {'box','tx'}, dimensions={0} | all-to-all | bytes 524288 | tf_op jit(solution)/shard_map/all_to_all | solution.py:445
  26.1 0.3 leaf_order.1
  26.4 10.5 %all_to_all.11.leaves_ref = bf16[16,32,128]{2,1,0:T(8,128)(2,1)S(1)} all-to-all(bf16[16,32,128]{2,1,0:T(8,128)(2,1)S(1)} %leaf_order.1), channel_id=1, replica_groups=mesh['box'=16,'tx'=2] {'box'}, dimensions={0} | all-to-all | bytes 262144 | tf_op jit(solution)/shard_map/all_to_all | solution.py:447
  37.0 1.9 %local_levels.1._.own_ref = bf16[32,16,128]{2,1,0:T(8,128)(2,1)S(1)} custom-call(bf16[16,32,128]{2,1,0:T(8,128)(2,1)S(1)} %all_to_all.11.leaves_ref, bf16[9,32,64,128]{3,2,1,0:T(8,128)(2,1)S(1)} %copy-done, bf16[9,32,64,128]{3,2,1,0:T(8,128)(2,1)S(1)} %copy-done.1), custom_call_target="tpu_custom_call" | custom-call | tf_op jit(solution)/shard_map/local_levels/pallas_call | solution.py:260
  38.8 0.1 collective-permute-start
  38.9 0.6 turn_factors.4.turned_ref
  39.5 0.8 %collective-permute-done.other_ref = bf16[32,16,128]{2,1,0:T(8,128)(2,1)S(1)} collective-permute-done((bf16[32,16,128]{2,1,0:T(8,128)(2,1)S(1)}, bf16[32,16,128]{2,1,0:T(8,128)(2,1)S(1)}, u32[]{:S(2)}, u32[]{:S(2)}) %collective-permute-start) | collective-permute-done | bytes 131104 | tf_op jit(solution)/shard_map/ppermute | solution.py:456
  40.2 0.4 pair_level.3._.own_ref
  40.7 0.1 collective-permute-start.1
  40.8 0.6 turn_factors.5.turned_ref
  41.3 5.0 %collective-permute-done.1.other_ref = bf16[32,16,128]{2,1,0:T(8,128)(2,1)S(1)} collective-permute-done((bf16[32,16,128]{2,1,0:T(8,128)(2,1)S(1)}, bf16[32,16,128]{2,1,0:T(8,128)(2,1)S(1)}, u32[]{:S(2)}, u32[]{:S(2)}) %collective-permute-start.1) | collective-permute-done | bytes 131104 | tf_op jit(solution)/shard_map/ppermute | solution.py:456
  46.3 0.4 pair_level.4._.own_ref
  46.7 0.1 collective-permute-start.2
  46.8 0.0 slice-start
  46.8 0.6 turn_factors.6.turned_ref
  47.4 0.0 slice-start.2
  47.4 4.3 %collective-permute-done.2.other_ref = bf16[32,16,128]{2,1,0:T(8,128)(2,1)S(1)} collective-permute-done((bf16[32,16,128]{2,1,0:T(8,128)(2,1)S(1)}, bf16[32,16,128]{2,1,0:T(8,128)(2,1)S(1)}, u32[]{:S(2)}, u32[]{:S(2)}) %collective-permute-start.2) | collective-permute-done | bytes 131104 | tf_op jit(solution)/shard_map/ppermute | solution.py:456
  51.7 0.4 pair_level.5._.own_ref
  52.2 0.0 slice-start.3
  52.2 0.4 collective-permute-start.3
  52.6 0.6 turn_factors.7.turned_ref
  53.1 6.1 %collective-permute-done.3.other_ref = bf16[32,16,128]{2,1,0:T(8,128)(2,1)S(1)} collective-permute-done((bf16[32,16,128]{2,1,0:T(8,128)(2,1)S(1)}, bf16[32,16,128]{2,1,0:T(8,128)(2,1)S(1)}, u32[]{:S(2)}, u32[]{:S(2)}) %collective-permute-start.3) | collective-permute-done | bytes 131104 | tf_op jit(solution)/shard_map/ppermute | solution.py:456
  59.3 3.6 %last_level_and_field.1 = bf16[32,16,4096]{2,1,0:T(8,128)(2,1)} custom-call(bf16[32,16,128]{2,1,0:T(8,128)(2,1)S(1)} %pair_level.5._.own_ref, bf16[32,16,128]{2,1,0:T(8,128)(2,1)S(1)} %collective-permute-done.3.other_ref, bf16[9,32,64,128]{3,2,1,0:T(8,128)(2,1)S(1)} %copy-done, bf16[9,32,64,128]{3,2,1,0:T(8,128)(2,1)S(1)} %copy-done.1, ...), custom_call_target="tpu_custom_call" | custom-call | tf_op jit(solution)/shard_map/last_level_and_field/pallas_call | solution.py:414
  (10 shorter events, 0.0 us)
Async XLA Ops:
  0.0 37.0 %copy-start = (bf16[9,32,64,128]{3,2,1,0:T(8,128)(2,1)S(1)}, bf16[9,32,64,128]{3,2,1,0:T(8,128)(2,1)}, u32[]{:S(2)}) copy-start(bf16[9,32,64,128]{3,2,1,0:T(8,128)(2,1)} %self_ref.17) | copy-start | bytes 14155780
  0.0 37.0 %copy-start.1 = (bf16[9,32,64,128]{3,2,1,0:T(8,128)(2,1)S(1)}, bf16[9,32,64,128]{3,2,1,0:T(8,128)(2,1)}, u32[]{:S(2)}) copy-start(bf16[9,32,64,128]{3,2,1,0:T(8,128)(2,1)} %cross_ref.17) | copy-start | bytes 14155780
  38.8 1.4 %collective-permute-start = (bf16[32,16,128]{2,1,0:T(8,128)(2,1)S(1)}, bf16[32,16,128]{2,1,0:T(8,128)(2,1)S(1)}, u32[]{:S(2)}, u32[]{:S(2)}) collective-permute-start(bf16[32,16,128]{2,1,0:T(8,128)(2,1)S(1)} %local_levels.1._.own_ref), channel_id=1, source_target_pairs={{0,2},{2,0},{4,6},{6,4},{8,10},{10,8},{12,14},{14,12},{16,18},{18,... | collective-permute-start | bytes 393224 | tf_op jit(solution)/shard_map/ppermute | solution.py:456
  40.7 5.6 %collective-permute-start.1 = (bf16[32,16,128]{2,1,0:T(8,128)(2,1)S(1)}, bf16[32,16,128]{2,1,0:T(8,128)(2,1)S(1)}, u32[]{:S(2)}, u32[]{:S(2)}) collective-permute-start(bf16[32,16,128]{2,1,0:T(8,128)(2,1)S(1)} %pair_level.3._.own_ref), channel_id=1, source_target_pairs={{0,4},{2,6},{4,0},{6,2},{8,12},{10,14},{12,8},{14,10},{16,20},{18,... | collective-permute-start | bytes 393224 | tf_op jit(solution)/shard_map/ppermute | solution.py:456
  46.7 5.0 %collective-permute-start.2 = (bf16[32,16,128]{2,1,0:T(8,128)(2,1)S(1)}, bf16[32,16,128]{2,1,0:T(8,128)(2,1)S(1)}, u32[]{:S(2)}, u32[]{:S(2)}) collective-permute-start(bf16[32,16,128]{2,1,0:T(8,128)(2,1)S(1)} %pair_level.4._.own_ref), channel_id=1, source_target_pairs={{0,8},{2,10},{4,12},{6,14},{8,0},{10,2},{12,4},{14,6},{16,24},{18,... | collective-permute-start | bytes 393224 | tf_op jit(solution)/shard_map/ppermute | solution.py:456
  46.8 12.5 %slice-start = ((s8[16777216]{0:T(1024)(128)(4,1)}), s8[4194304]{0:T(1024)(128)(4,1)S(1)}, s32[]{:S(2)}) async-start(s8[16777216]{0:T(1024)(128)(4,1)} %bitcast.2), calls=%async_computation.2 | async-start | bytes 8388608
  46.8 12.5 %slice-start.1 = ((s8[16777216]{0:T(1024)(128)(4,1)}), s8[4194304]{0:T(1024)(128)(4,1)S(1)}, s32[]{:S(2)}) async-start(s8[16777216]{0:T(1024)(128)(4,1)} %bitcast.2), calls=%async_computation.3 | async-start | bytes 8388608
  47.4 11.9 %slice-start.2 = ((s8[16777216]{0:T(1024)(128)(4,1)}), s8[4194304]{0:T(1024)(128)(4,1)S(1)}, s32[]{:S(2)}) async-start(s8[16777216]{0:T(1024)(128)(4,1)} %bitcast.2), calls=%async_computation.4 | async-start | bytes 8388608
  52.2 7.1 %slice-start.3 = ((s8[16777216]{0:T(1024)(128)(4,1)}), s8[4194304]{0:T(1024)(128)(4,1)S(1)}, s32[]{:S(2)}) async-start(s8[16777216]{0:T(1024)(128)(4,1)} %bitcast.2), calls=%async_computation.5 | async-start | bytes 8388608
  52.2 7.1 %collective-permute-start.3 = (bf16[32,16,128]{2,1,0:T(8,128)(2,1)S(1)}, bf16[32,16,128]{2,1,0:T(8,128)(2,1)S(1)}, u32[]{:S(2)}, u32[]{:S(2)}) collective-permute-start(bf16[32,16,128]{2,1,0:T(8,128)(2,1)S(1)} %pair_level.5._.own_ref), channel_id=1, source_target_pairs={{0,16},{2,18},{4,20},{6,22},{8,24},{10,26},{12,28},{14,30},{16,0},... | collective-permute-start | bytes 393224 | tf_op jit(solution)/shard_map/ppermute | solution.py:456

commit v5 on v4

--- a/solution.py
+++ b/solution.py
@@ -84,7 +84,7 @@
     pick_copy.start()
     slot_copy.start()
     for g in range(2):
-        leaf_copy(g).start()
+        leaf_copy(g).start(priority=1)
     pick_copy.wait()
     for k in range(row_groups):
         present[k] = 0
@@ -104,7 +104,7 @@
     for g in range(batches):
         lax.fori_loop(0, count, lambda j, _, g=g: (bank_copy(g, j).start(), 0)[1], 0)
         if g > 1:
-            leaf_copy(g).start()
+            leaf_copy(g).start(priority=1)
 
     row = lax.broadcasted_iota(jnp.int32, (picked, stored), 0)
     column = lax.broadcasted_iota(jnp.int32, (picked, stored), 1)
@@ -337,8 +337,8 @@
     )(own, other, self_factor, cross_factor, turned)
 
 
-GROUP = 4
-TILE = 512
+GROUP = 2
+TILE = 2048
 
 
 def field_kernel(
@@ -356,6 +356,7 @@
     slots, cols, rank2 = own_ref.shape
     rank = rank2 // 2
     points = target_ref.shape[-1] // 2
+    tile = min(TILE, points)
     for i in range(0, slots, 2):
         pair = mix_pair(level, offset, i, own_ref, other_ref, self_ref, cross_ref, turned_ref)
         final[i] = pair[0]
@@ -381,17 +382,17 @@
             )
         rows = jnp.concatenate(rows, axis=0).astype(BF16)
         part = pl.ds(offset + q * GROUP, GROUP)
-        for start in range(0, points, TILE):
-            real_part = target_ref[part, :, pl.ds(start, TILE)].reshape(GROUP * rank, TILE)
-            imag_part = target_ref[part, :, pl.ds(points + start, TILE)].reshape(GROUP * rank, TILE)
+        for start in range(0, points, tile):
+            real_part = target_ref[part, :, pl.ds(start, tile)].reshape(GROUP * rank, tile)
+            imag_part = target_ref[part, :, pl.ds(points + start, tile)].reshape(GROUP * rank, tile)
             by_real = dot(rows, real_part)
             by_imag = dot(rows, imag_part)
             for i in range(GROUP):
                 xr = slice(2 * cols * i, 2 * cols * i + cols)
                 xi = slice(2 * cols * i + cols, 2 * cols * (i + 1))
                 box = q * GROUP + i
-                result[box, :, pl.ds(start, TILE)] = (by_real[xr] - by_imag[xi]).astype(BF16)
-                result[box, :, pl.ds(points + start, TILE)] = (by_imag[xr] + by_real[xi]).astype(BF16)
+                result[box, :, pl.ds(start, tile)] = (by_real[xr] - by_imag[xi]).astype(BF16)
+                result[box, :, pl.ds(points + start, tile)] = (by_imag[xr] + by_real[xi]).astype(BF16)
         out_copy(q).start()
 
     for q in range(slots // GROUP):

time: 63.4 us -> 63.2 us (level)
  no operation moved by 1% of the time
where the time goes in v5:
time: 63.2 us; the launch traced here: 63.1 us
  blocking collectives  28.7 us (45%)
  Pallas kernels  17.2 us (27%)
  waiting for transfers between devices  16.2 us (26%)
    all_to_all x1, blocking collectives, per_device(): sent = lax.all_to_all(sent, ('box', 'tx'), 0, 0, tiled=True)  18.2 us
    ppermute x4, waiting for transfers between devices, per_device(): others = [lax.ppermute(part, 'box', route) for part in current]  16.2 us
    all_to_all x1, blocking collectives, per_device(): leaves = lax.all_to_all(ordered, 'box', 0, 0, tiled=True)  10.5 us
    pallas_call x1, Pallas kernels, leaf_step(): pl.pallas_call(functools.partial(leaf_kernel, cols), out_shape=(jax.Shape...  8.07 us
    pallas_call x1, Pallas kernels, field_step(): pl.pallas_call(functools.partial(field_kernel, level, offset), out_shape=...  3.52 us
    pallas_call x4, Pallas kernels, turn_step(): pl.pallas_call(functools.partial(turn_kernel, level), out_shape=jax.Shape...  2.25 us
    pallas_call x1, Pallas kernels, local_step(): pl.pallas_call(functools.partial(local_kernel, local_bits), out_shape=jax...  1.87 us
  transfers between devices with their start and end apart: 4, of which 4 were waited for; matrix products, arithmetic and copies ran while one was open for 0% of the time, Pallas kernels for 4%

profile of v5, /device:TPU:0, one launch (start us, length us, event | category | flops | bytes accessed | tf_op | source)
XLA Modules:
  0.0 63.1 jit_solution(15163570884577330857)
XLA Ops:
  0.0 8.1 %select_and_leaf.1 = (bf16[32,32,128]{2,1,0:T(8,128)(2,1)S(1)}, bf16[512,512]{1,0:T(8,128)(2,1)S(1)}) custom-call(s32[32]{0:T(128)} %pick_hbm.1, s32[1,512]{1,0:T(1,128)} %bitcast.5, bf16[32,256,1024]{2,1,0:T(8,128)(2,1)} %bank_ref.1, bf16[32,512,128]{2,1,0:T(8,128)(2,1)} %leaf_ref.1), custom_call_target="tpu_custom_call" | custom-call | tf_op jit(solution)/shard_map/select_and_leaf/pallas_call | solution.py:174
  8.1 18.2 %all_to_all.10 = bf16[32,32,128]{2,1,0:T(8,128)(2,1)S(1)} all-to-all(bf16[32,32,128]{2,1,0:T(8,128)(2,1)S(1)} %get-tuple-element.8), channel_id=1, replica_groups=mesh['box'=16,'tx'=2] {'box','tx'}, dimensions={0} | all-to-all | bytes 524288 | tf_op jit(solution)/shard_map/all_to_all | solution.py:446
  26.3 0.3 leaf_order.1
  26.6 10.5 %all_to_all.11.leaves_ref = bf16[16,32,128]{2,1,0:T(8,128)(2,1)S(1)} all-to-all(bf16[16,32,128]{2,1,0:T(8,128)(2,1)S(1)} %leaf_order.1), channel_id=1, replica_groups=mesh['box'=16,'tx'=2] {'box'}, dimensions={0} | all-to-all | bytes 262144 | tf_op jit(solution)/shard_map/all_to_all | solution.py:448
  37.1 1.9 %local_levels.1._.own_ref = bf16[32,16,128]{2,1,0:T(8,128)(2,1)S(1)} custom-call(bf16[16,32,128]{2,1,0:T(8,128)(2,1)S(1)} %all_to_all.11.leaves_ref, bf16[9,32,64,128]{3,2,1,0:T(8,128)(2,1)S(1)} %copy-done, bf16[9,32,64,128]{3,2,1,0:T(8,128)(2,1)S(1)} %copy-done.1), custom_call_target="tpu_custom_call" | custom-call | tf_op jit(solution)/shard_map/local_levels/pallas_call | solution.py:260
  39.0 0.1 collective-permute-start
  39.1 0.6 turn_factors.4.turned_ref
  39.6 0.8 %collective-permute-done.other_ref = bf16[32,16,128]{2,1,0:T(8,128)(2,1)S(1)} collective-permute-done((bf16[32,16,128]{2,1,0:T(8,128)(2,1)S(1)}, bf16[32,16,128]{2,1,0:T(8,128)(2,1)S(1)}, u32[]{:S(2)}, u32[]{:S(2)}) %collective-permute-start) | collective-permute-done | bytes 131104 | tf_op jit(solution)/shard_map/ppermute | solution.py:457
  40.4 0.4 pair_level.3._.own_ref
  40.8 0.1 collective-permute-start.1
  40.9 0.6 turn_factors.5.turned_ref
  41.5 5.0 %collective-permute-done.1.other_ref = bf16[32,16,128]{2,1,0:T(8,128)(2,1)S(1)} collective-permute-done((bf16[32,16,128]{2,1,0:T(8,128)(2,1)S(1)}, bf16[32,16,128]{2,1,0:T(8,128)(2,1)S(1)}, u32[]{:S(2)}, u32[]{:S(2)}) %collective-permute-start.1) | collective-permute-done | bytes 131104 | tf_op jit(solution)/shard_map/ppermute | solution.py:457
  46.4 0.4 pair_level.4._.own_ref
  46.9 0.1 collective-permute-start.2
  46.9 0.0 slice-start
  47.0 0.6 turn_factors.6.turned_ref
  47.5 0.0 slice-start.2
  47.5 4.3 %collective-permute-done.2.other_ref = bf16[32,16,128]{2,1,0:T(8,128)(2,1)S(1)} collective-permute-done((bf16[32,16,128]{2,1,0:T(8,128)(2,1)S(1)}, bf16[32,16,128]{2,1,0:T(8,128)(2,1)S(1)}, u32[]{:S(2)}, u32[]{:S(2)}) %collective-permute-start.2) | collective-permute-done | bytes 131104 | tf_op jit(solution)/shard_map/ppermute | solution.py:457
  51.9 0.4 pair_level.5._.own_ref
  52.3 0.0 slice-start.3
  52.3 0.4 collective-permute-start.3
  52.7 0.6 turn_factors.7.turned_ref
  53.3 6.1 %collective-permute-done.3.other_ref = bf16[32,16,128]{2,1,0:T(8,128)(2,1)S(1)} collective-permute-done((bf16[32,16,128]{2,1,0:T(8,128)(2,1)S(1)}, bf16[32,16,128]{2,1,0:T(8,128)(2,1)S(1)}, u32[]{:S(2)}, u32[]{:S(2)}) %collective-permute-start.3) | collective-permute-done | bytes 131104 | tf_op jit(solution)/shard_map/ppermute | solution.py:457
  59.4 3.5 %last_level_and_field.1 = bf16[32,16,4096]{2,1,0:T(8,128)(2,1)} custom-call(bf16[32,16,128]{2,1,0:T(8,128)(2,1)S(1)} %pair_level.5._.own_ref, bf16[32,16,128]{2,1,0:T(8,128)(2,1)S(1)} %collective-permute-done.3.other_ref, bf16[9,32,64,128]{3,2,1,0:T(8,128)(2,1)S(1)} %copy-done, bf16[9,32,64,128]{3,2,1,0:T(8,128)(2,1)S(1)} %copy-done.1, ...), custom_call_target="tpu_custom_call" | custom-call | tf_op jit(solution)/shard_map/last_level_and_field/pallas_call | solution.py:415
  (10 shorter events, 0.0 us)
Async XLA Ops:
  0.0 37.1 %copy-start = (bf16[9,32,64,128]{3,2,1,0:T(8,128)(2,1)S(1)}, bf16[9,32,64,128]{3,2,1,0:T(8,128)(2,1)}, u32[]{:S(2)}) copy-start(bf16[9,32,64,128]{3,2,1,0:T(8,128)(2,1)} %self_ref.17) | copy-start | bytes 14155780
  0.0 37.1 %copy-start.1 = (bf16[9,32,64,128]{3,2,1,0:T(8,128)(2,1)S(1)}, bf16[9,32,64,128]{3,2,1,0:T(8,128)(2,1)}, u32[]{:S(2)}) copy-start(bf16[9,32,64,128]{3,2,1,0:T(8,128)(2,1)} %cross_ref.17) | copy-start | bytes 14155780
  39.0 1.4 %collective-permute-start = (bf16[32,16,128]{2,1,0:T(8,128)(2,1)S(1)}, bf16[32,16,128]{2,1,0:T(8,128)(2,1)S(1)}, u32[]{:S(2)}, u32[]{:S(2)}) collective-permute-start(bf16[32,16,128]{2,1,0:T(8,128)(2,1)S(1)} %local_levels.1._.own_ref), channel_id=1, source_target_pairs={{0,2},{2,0},{4,6},{6,4},{8,10},{10,8},{12,14},{14,12},{16,18},{18,... | collective-permute-start | bytes 393224 | tf_op jit(solution)/shard_map/ppermute | solution.py:457
  40.8 5.6 %collective-permute-start.1 = (bf16[32,16,128]{2,1,0:T(8,128)(2,1)S(1)}, bf16[32,16,128]{2,1,0:T(8,128)(2,1)S(1)}, u32[]{:S(2)}, u32[]{:S(2)}) collective-permute-start(bf16[32,16,128]{2,1,0:T(8,128)(2,1)S(1)} %pair_level.3._.own_ref), channel_id=1, source_target_pairs={{0,4},{2,6},{4,0},{6,2},{8,12},{10,14},{12,8},{14,10},{16,20},{18,... | collective-permute-start | bytes 393224 | tf_op jit(solution)/shard_map/ppermute | solution.py:457
  46.9 5.0 %collective-permute-start.2 = (bf16[32,16,128]{2,1,0:T(8,128)(2,1)S(1)}, bf16[32,16,128]{2,1,0:T(8,128)(2,1)S(1)}, u32[]{:S(2)}, u32[]{:S(2)}) collective-permute-start(bf16[32,16,128]{2,1,0:T(8,128)(2,1)S(1)} %pair_level.4._.own_ref), channel_id=1, source_target_pairs={{0,8},{2,10},{4,12},{6,14},{8,0},{10,2},{12,4},{14,6},{16,24},{18,... | collective-permute-start | bytes 393224 | tf_op jit(solution)/shard_map/ppermute | solution.py:457
  46.9 12.5 %slice-start = ((s8[16777216]{0:T(1024)(128)(4,1)}), s8[4194304]{0:T(1024)(128)(4,1)S(1)}, s32[]{:S(2)}) async-start(s8[16777216]{0:T(1024)(128)(4,1)} %bitcast.2), calls=%async_computation.2 | async-start | bytes 8388608
  46.9 12.5 %slice-start.1 = ((s8[16777216]{0:T(1024)(128)(4,1)}), s8[4194304]{0:T(1024)(128)(4,1)S(1)}, s32[]{:S(2)}) async-start(s8[16777216]{0:T(1024)(128)(4,1)} %bitcast.2), calls=%async_computation.3 | async-start | bytes 8388608
  47.5 11.9 %slice-start.2 = ((s8[16777216]{0:T(1024)(128)(4,1)}), s8[4194304]{0:T(1024)(128)(4,1)S(1)}, s32[]{:S(2)}) async-start(s8[16777216]{0:T(1024)(128)(4,1)} %bitcast.2), calls=%async_computation.4 | async-start | bytes 8388608
  52.3 7.1 %slice-start.3 = ((s8[16777216]{0:T(1024)(128)(4,1)}), s8[4194304]{0:T(1024)(128)(4,1)S(1)}, s32[]{:S(2)}) async-start(s8[16777216]{0:T(1024)(128)(4,1)} %bitcast.2), calls=%async_computation.5 | async-start | bytes 8388608
  52.3 7.1 %collective-permute-start.3 = (bf16[32,16,128]{2,1,0:T(8,128)(2,1)S(1)}, bf16[32,16,128]{2,1,0:T(8,128)(2,1)S(1)}, u32[]{:S(2)}, u32[]{:S(2)}) collective-permute-start(bf16[32,16,128]{2,1,0:T(8,128)(2,1)S(1)} %pair_level.5._.own_ref), channel_id=1, source_target_pairs={{0,16},{2,18},{4,20},{6,22},{8,24},{10,26},{12,28},{14,30},{16,0},... | collective-permute-start | bytes 393224 | tf_op jit(solution)/shard_map/ppermute | solution.py:457
